TPU v7x, 32 devices: a whole 2x2x4 slice. The times are simulated.
32 devices in a mesh: rep: 2 (over y), exp: 16 (over z, x, core).
Axes of the slice: x: 2, y: 2, z: 4, core: 2. Of those that a mesh axis runs over, the one named last changes fastest.
Arguments:
- tokens: bfloat16 [2, 768, 2048], P(None, ('rep', 'exp')), may hold values from -6 to 6
- cotangent: bfloat16 [2, 768, 2048], P(None, ('rep', 'exp')), may hold values from -12 to 12
- routes: int32 [2, 768, 8], P(None, ('rep', 'exp')), may hold values from 0 to 15, all different within a row; in each aligned block of 24 rows (0 to 23, 24 to 47, ..., all dimensions but the last counted through in order) at most 16 rows name the same one
- gates: bfloat16 [2, 768, 8], P(None, ('rep', 'exp')), may hold values from 0.049804688 to 0.34960938
- collapsed: int32 [16], P('exp'), may hold values 0 or 1
- w_in: bfloat16 [16, 2048, 1536], P('exp', 'rep'), may hold values from -5 to 5
- w_out: bfloat16 [16, 768, 2048], P('exp', 'rep'), may hold values from -5 to 5
- first_in: bfloat16 [16, 2048, 1536], P('exp', 'rep'), may hold values from -2 to 2
- second_in: bfloat16 [16, 2048, 1536], P('exp', 'rep'), may hold values from 0.0099487305 to 1
- first_out: bfloat16 [16, 768, 2048], P('exp', 'rep'), may hold values from -2 to 2
- second_out: bfloat16 [16, 768, 2048], P('exp', 'rep'), may hold values from 0.0099487305 to 1
- fresh_in: bfloat16 [16, 2048, 1536], P('exp', 'rep'), may hold values from -5 to 5
- fresh_out: bfloat16 [16, 768, 2048], P('exp', 'rep'), may hold values from -5 to 5
Outputs:
- d_tokens: bfloat16 [2, 768, 2048], P(None, ('rep', 'exp'))
- d_gates: bfloat16 [2, 768, 8], P(None, ('rep', 'exp'))
- new_w_in: bfloat16 [16, 2048, 1536], P('exp', 'rep')
- new_w_out: bfloat16 [16, 768, 2048], P('exp', 'rep')
- new_first_in: bfloat16 [16, 2048, 1536], P('exp', 'rep')
- new_second_in: bfloat16 [16, 2048, 1536], P('exp', 'rep')
- new_first_out: bfloat16 [16, 768, 2048], P('exp', 'rep')
- new_second_out: bfloat16 [16, 768, 2048], P('exp', 'rep')
Inputs may be any that keep to these rules, and one draw needn't show every extreme that they name: `routes`: in each microbatch the 24 tokens of one device name no expert more than 16 times, and some device names some expert exactly 16 times; a token names 8 different experts.
All inputs are finite; a program needn't handle non-finite values. No bound on the sum of `collapsed` on one device may be relied on, other than what follows from the above.
Results may differ from a plain program's by a relative error of at most 0.0085.
Values may be sent and summed in bfloat16 or wider, within the bound.
A program may use at most 128 MiB of HBM per device.

v0:
```python
import math

import jax
import jax.numpy as jnp
from jax import lax
from jax.sharding import PartitionSpec as P

beta_one = 0.9
beta_two = 0.95
learn_rate = 0.01
adam_eps = 1e-08
adam_count = 10.0


def silu_parts(gate_half):
    sigmoid_val = jax.nn.sigmoid(gate_half)
    return (gate_half * sigmoid_val, sigmoid_val * (1.0 + gate_half * (1.0 - sigmoid_val)))


def expert_front(rows_in, rows_cot, rows_gate, weight_in, weight_out, scale_in, scale_out):
    hidden = weight_out.shape[0]
    pre_act = jnp.dot(rows_in, weight_in, preferred_element_type=jnp.float32) * scale_in
    gate_half = pre_act[:, :hidden]
    up_half = pre_act[:, hidden:]
    silu_val, slope_val = silu_parts(gate_half)
    active = (silu_val * up_half).astype(jnp.bfloat16)
    result = jnp.dot(active, weight_out, preferred_element_type=jnp.float32) * scale_out
    gate_grad = jnp.sum(rows_cot.astype(jnp.float32) * result, axis=1)
    out_cot = (rows_gate.astype(jnp.float32)[:, None] * rows_cot.astype(jnp.float32)).astype(
        jnp.bfloat16
    )
    act_cot = (
        lax.dot_general(
            out_cot, weight_out, (((1,), (1,)), ((), ())), preferred_element_type=jnp.float32
        )
        * scale_out
    )
    return (up_half, silu_val, slope_val, act_cot, gate_grad, active, out_cot)


def expert_back(up_half, silu_val, slope_val, act_cot, weight_in, scale_in):
    pre_cot = jnp.concatenate([act_cot * up_half * slope_val, act_cot * silu_val], axis=1).astype(
        jnp.bfloat16
    )
    rows_dx = (
        lax.dot_general(
            pre_cot, weight_in, (((1,), (1,)), ((), ())), preferred_element_type=jnp.float32
        )
        * scale_in
    ).astype(jnp.bfloat16)
    return (pre_cot, rows_dx)


def adam_update(weight, first, second, grad, fresh, dead_flag):
    first_new = beta_one * first.astype(jnp.float32) + (1.0 - beta_one) * grad
    second_new = beta_two * second.astype(jnp.float32) + (1.0 - beta_two) * grad * grad
    first_hat = first_new / (1.0 - beta_one**adam_count)
    second_hat = second_new / (1.0 - beta_two**adam_count)
    stepped = weight.astype(jnp.float32) - learn_rate * first_hat / (
        jnp.sqrt(second_hat) + adam_eps
    )
    alive_mask = dead_flag == 0
    return (
        jnp.where(alive_mask, stepped, fresh.astype(jnp.float32)).astype(jnp.bfloat16),
        jnp.where(alive_mask, first_new, jnp.zeros_like(first_new)).astype(jnp.bfloat16),
        jnp.where(alive_mask, second_new, jnp.zeros_like(second_new)).astype(jnp.bfloat16),
    )


def dispatch_match(route_rows, num_exp, capacity):
    flat_routes = route_rows.reshape(-1)
    onehot = (flat_routes[:, None] == jnp.arange(num_exp, dtype=jnp.int32)[None, :]).astype(
        jnp.int32
    )
    slot_rank = jnp.sum((jnp.cumsum(onehot, axis=0) - onehot) * onehot, axis=1)
    target = (flat_routes * capacity + slot_rank).reshape(route_rows.shape)
    return target[None, :, :] == jnp.arange(num_exp * capacity, dtype=jnp.int32)[:, None, None]


def pack_rows(matched, picker, token_rows, cot_rows, gate_rows, num_exp, capacity):
    sent_in = jnp.dot(picker, token_rows, preferred_element_type=jnp.float32).astype(jnp.bfloat16)
    sent_cot = jnp.dot(picker, cot_rows, preferred_element_type=jnp.float32).astype(jnp.bfloat16)
    sent_gate = jnp.sum(
        jnp.where(matched, gate_rows[None, :, :].astype(jnp.float32), 0.0), axis=(1, 2)
    ).astype(jnp.bfloat16)
    return (
        sent_in.reshape(num_exp, capacity, -1),
        sent_cot.reshape(num_exp, capacity, -1),
        sent_gate.reshape(num_exp, capacity),
    )


def body(
    tokens,
    cotangent,
    routes,
    gates,
    collapsed,
    w_in,
    w_out,
    first_in,
    second_in,
    first_out,
    second_out,
    fresh_in,
    fresh_out,
):
    micro_count, tok_rows, model_width = tokens.shape
    route_width = routes.shape[2]
    sources = lax.axis_size("exp")
    num_exp = w_in.shape[0] * sources
    capacity = min(tok_rows, (4 * tok_rows * route_width + 3 * num_exp - 1) // (3 * num_exp))
    full_in, full_out = (
        lax.all_gather(w_in, "rep", axis=1, tiled=True),
        lax.all_gather(w_out, "rep", axis=1, tiled=True),
    )
    weight_in = full_in[0]
    weight_out = full_out[0]
    hidden = weight_out.shape[0]
    scale_in = 1.0 / math.sqrt(model_width)
    scale_out = 1.0 / math.sqrt(hidden)
    matches = [
        dispatch_match(routes[which_micro], num_exp, capacity) for which_micro in range(micro_count)
    ]
    pickers = [jnp.any(matched, axis=2).astype(jnp.bfloat16) for matched in matches]
    packs = [
        pack_rows(
            matches[which_micro],
            pickers[which_micro],
            tokens[which_micro],
            cotangent[which_micro],
            gates[which_micro],
            num_exp,
            capacity,
        )
        for which_micro in range(micro_count)
    ]
    joined = [jnp.concatenate([packed[member] for packed in packs], axis=1) for member in range(3)]
    arrived = (
        lax.all_to_all(joined[0], "exp", split_axis=0, concat_axis=0, tiled=True),
        lax.all_to_all(joined[1], "exp", split_axis=0, concat_axis=0, tiled=True),
        lax.all_to_all(joined[2], "exp", split_axis=0, concat_axis=0, tiled=True),
    )
    rows_in = arrived[0].reshape(-1, model_width)
    rows_cot = arrived[1].reshape(-1, model_width)
    rows_gate = arrived[2].reshape(-1)
    front_vals = expert_front(
        rows_in, rows_cot, rows_gate, weight_in, weight_out, scale_in, scale_out
    )
    grad_out = (
        lax.dot_general(
            front_vals[5],
            front_vals[6],
            (((0,), (0,)), ((), ())),
            preferred_element_type=jnp.float32,
        )
        * scale_out
    )
    fronts = (rows_in, front_vals)
    rows_in, front_vals = fronts
    pre_cot, rows_dx = expert_back(
        front_vals[0], front_vals[1], front_vals[2], front_vals[3], weight_in, scale_in
    )
    grad_in = (
        lax.dot_general(
            rows_in, pre_cot, (((0,), (0,)), ((), ())), preferred_element_type=jnp.float32
        )
        * scale_in
    )
    back_vals = (rows_dx, front_vals[4].astype(jnp.bfloat16))
    summed_in, summed_out = (
        lax.psum_scatter(
            grad_in[None].astype(jnp.bfloat16), "rep", scatter_dimension=1, tiled=True
        ).astype(jnp.float32),
        lax.psum_scatter(
            grad_out[None].astype(jnp.bfloat16), "rep", scatter_dimension=1, tiled=True
        ).astype(jnp.float32),
    )
    rows_dx, gate_grad = back_vals
    returned = (
        lax.all_to_all(
            rows_dx.reshape(sources, -1, model_width),
            "exp",
            split_axis=0,
            concat_axis=0,
            tiled=True,
        ),
        lax.all_to_all(
            gate_grad.reshape(sources, -1), "exp", split_axis=0, concat_axis=0, tiled=True
        ),
    )
    parts_dx = returned[0].reshape(num_exp, micro_count, capacity, model_width)
    parts_gate = returned[1].reshape(num_exp, micro_count, capacity)
    results = [
        (parts_dx[:, which_micro].reshape(-1, model_width), parts_gate[:, which_micro].reshape(-1))
        for which_micro in range(micro_count)
    ]
    token_dx = []
    token_gate = []
    for which_micro in range(micro_count):
        token_dx.append(
            lax.dot_general(
                pickers[which_micro],
                results[which_micro][0],
                (((0,), (0,)), ((), ())),
                preferred_element_type=jnp.float32,
            ).astype(jnp.bfloat16)
        )
        token_gate.append(
            jnp.sum(
                jnp.where(
                    matches[which_micro],
                    results[which_micro][1].astype(jnp.float32)[:, None, None],
                    0.0,
                ),
                axis=0,
            ).astype(jnp.bfloat16)
        )
    dead_flag = collapsed.reshape(-1, 1, 1)
    updated_in = adam_update(w_in, first_in, second_in, summed_in, fresh_in, dead_flag)
    updated_out = adam_update(w_out, first_out, second_out, summed_out, fresh_out, dead_flag)
    return (
        jnp.stack(token_dx),
        jnp.stack(token_gate),
        updated_in[0],
        updated_out[0],
        updated_in[1],
        updated_in[2],
        updated_out[1],
        updated_out[2],
    )


def solution(mesh):
    placed = (
        P(None, ("rep", "exp"), None),
        P(None, ("rep", "exp"), None),
        P(None, ("rep", "exp"), None),
        P(None, ("rep", "exp"), None),
        P("exp"),
        P("exp", "rep", None),
        P("exp", "rep", None),
        P("exp", "rep", None),
        P("exp", "rep", None),
        P("exp", "rep", None),
        P("exp", "rep", None),
        P("exp", "rep", None),
        P("exp", "rep", None),
    )
    return jax.shard_map(
        body,
        mesh=mesh,
        in_specs=placed,
        out_specs=(
            P(None, ("rep", "exp"), None),
            P(None, ("rep", "exp"), None),
            P("exp", "rep", None),
            P("exp", "rep", None),
            P("exp", "rep", None),
            P("exp", "rep", None),
            P("exp", "rep", None),
            P("exp", "rep", None),
        ),
        check_vma=False,
    )
```

profile of v0, /device:TPU:0, one launch (start us, length us, event | category | flops | bytes accessed | tf_op | source)
XLA Modules:
  0.0 308.5 jit_solution(5969574759579811102)
XLA Ops:
  7.2 0.7 all-gather.5.cloned.1.call-update
  7.9 0.1 copy.76
  8.0 0.1 eq.90
  8.1 0.6 reduce-window.16
  8.7 0.2 slice_reduce_fusion
  8.9 0.1 bitcast_bitcast_fusion
  9.1 0.1 reduce_sum.71
  9.1 0.1 copy.75
  9.2 0.1 eq.79
  9.3 0.6 reduce-window.14
  9.9 0.2 slice_reduce_fusion.1
  10.3 0.1 reduce_sum.68
  10.4 0.1 fusion.27
  10.5 0.1 fusion.28
  10.7 0.5 convolution_convert_fusion
  11.2 0.5 convolution_convert_fusion.1
  11.6 1.6 pad_maximum_fusion.1
  13.2 7.4 %all-to-all-start.2 = ((bf16[16,32,2048]{2,1,0:T(8,128)(2,1)}), bf16[16,32,2048]{2,1,0:T(8,128)(2,1)S(1)}, u32[]{:S(2)}, u32[]{:S(2)}) async-start(bf16[16,32,2048]{2,1,0:T(8,128)(2,1)} %pad_maximum_fusion.1), calls=%async_computation.2 | async-start | bytes 4194304 | tf_op jit(solution)/shard_map/all_to_all | solution.py:140
  20.6 0.5 convolution_convert_fusion.2
  21.1 0.5 convolution_convert_fusion.3
  21.6 1.6 pad_maximum_fusion
  23.1 38.6 %all-to-all-done.2 = bf16[16,32,2048]{2,1,0:T(8,128)(2,1)S(1)} async-done(((bf16[16,32,2048]{2,1,0:T(8,128)(2,1)}), bf16[16,32,2048]{2,1,0:T(8,128)(2,1)S(1)}, u32[]{:S(2)}, u32[]{:S(2)}) %all-to-all-start.2) | async-done | bytes 2097184 | tf_op jit(solution)/shard_map/all_to_all | solution.py:140
  61.7 1.3 copy-done.3
  63.0 11.2 %all-to-all-start.1 = ((bf16[16,32,2048]{2,1,0:T(8,128)(2,1)}), bf16[16,32,2048]{2,1,0:T(8,128)(2,1)S(1)}, u32[]{:S(2)}, u32[]{:S(2)}) async-start(bf16[16,32,2048]{2,1,0:T(8,128)(2,1)} %pad_maximum_fusion), calls=%async_computation.1 | async-start | bytes 4194304 | tf_op jit(solution)/shard_map/all_to_all | solution.py:141
  74.3 0.7 all-gather.3.cloned.1.call-update
  75.0 17.7 %all-gather.5.cloned.1.call-done = bf16[1,2048,1536]{2,1,0:T(8,128)(2,1)} async-done(((bf16[1,1024,1536]{2,1,0:T(8,128)(2,1)}), bf16[1,2048,1536]{2,1,0:T(8,128)(2,1)}) %all-gather.5.cloned.1.call-update) | async-done | bytes 6291472 | tf_op jit(solution)/shard_map/all_gather | solution.py:114
  92.7 6.2 %fusion.10 = f32[512,1536]{1,0:T(8,128)S(1)} fusion(bf16[512,2048]{1,0:T(8,128)(2,1)} %bitcast.120, bf16[1,2048,1536]{2,1,0:T(8,128)(2,1)} %all-gather.5.cloned.1.call-done), kind=kOutput, calls=%fused_computation.23 | convolution fusion | flops 3222011904 | bytes 11534336 | tf_op jit(solution)/shard_map/dot_general | solution.py:22
  98.9 1.7 copy-done.1
  100.6 0.5 multiply_convert_fusion.3
  101.1 38.2 %all-gather.3.cloned.1.call-done = bf16[1,768,2048]{2,1,0:T(8,128)(2,1)} async-done(((bf16[1,384,2048]{2,1,0:T(8,128)(2,1)}), bf16[1,768,2048]{2,1,0:T(8,128)(2,1)}) %all-gather.3.cloned.1.call-update) | async-done | bytes 3145744 | tf_op jit(solution)/shard_map/all_gather | solution.py:115
  139.2 3.8 %fusion.8 = bf16[512]{0:T(512)(128)(2,1)S(1)} fusion(bf16[16,32,2048]{2,1,0:T(8,128)(2,1)S(1)} %all-to-all-done.1, bf16[512,768]{1,0:T(8,128)(2,1)S(1)} %multiply_convert_fusion.3, bf16[1,768,2048]{2,1,0:T(8,128)(2,1)} %all-gather.3.cloned.1.call-done), kind=kOutput, calls=%fused_computation.19 | convolution fusion | flops 1614806528 | bytes 6030336 | tf_op jit(solution)/shard_map/dot_general | solution.py:27
  143.0 0.7 convert_element_type.264
  143.7 5.6 %all-to-all-start.4 = ((bf16[16,1,32]{2,1,0:T(2,128)(2,1)}), bf16[16,1,32]{2,1,0:T(2,128)(2,1)S(1)}, u32[]{:S(2)}, u32[]{:S(2)}) async-start(bf16[16,1,32]{2,1,0:T(2,128)(2,1)} %convert_element_type.264), calls=%async_computation.4 | async-start | bytes 16384 | tf_op jit(solution)/shard_map/all_to_all | solution.py:188
  149.6 6.1 %all-to-all-done.4 = bf16[16,1,32]{2,1,0:T(2,128)(2,1)S(1)} async-done(((bf16[16,1,32]{2,1,0:T(2,128)(2,1)}), bf16[16,1,32]{2,1,0:T(2,128)(2,1)S(1)}, u32[]{:S(2)}, u32[]{:S(2)}) %all-to-all-start.4) | async-done | bytes 1056 | tf_op jit(solution)/shard_map/all_to_all | solution.py:188
  155.7 0.1 reshape.162
  155.9 0.1 reshape.170
  155.9 0.2 select_reduce_fusion
  156.1 0.1 convert_element_type.210
  156.2 0.1 reshape.169
  156.3 0.2 select_reduce_fusion.1
  156.5 0.1 convert_element_type.207
  156.6 0.1 maximum_bitcast_fusion
  156.7 9.0 %all_to_all.30 = bf16[16,1,32]{2,1,0:T(2,128)(2,1)S(1)} all-to-all(bf16[16,1,32]{2,1,0:T(2,128)(2,1)S(1)} %copy.71), channel_id=1, replica_groups=mesh['rep'=2,'exp'=16] {'exp'}, dimensions={0} | all-to-all | bytes 2048 | tf_op jit(solution)/shard_map/all_to_all | solution.py:142
  165.7 0.1 reshape.171
  165.8 0.4 fusion.9
  166.2 3.5 %fusion.20 = bf16[1,768,2048]{2,1,0:T(8,128)(2,1)} fusion(bf16[512,768]{1,0:T(8,128)(2,1)S(1)} %multiply_convert_fusion.3, bf16[512,2048]{1,0:T(8,128)(2,1)S(1)} %fusion.9), kind=kOutput, calls=%fused_computation.32 | convolution fusion | flops 1613758464 | bytes 6029312 | tf_op jit(solution)/shard_map/dot_general | solution.py:151
  169.7 0.2 reduce-scatter.3.cloned.1.call-start
  170.0 0.4 fusion.7
  170.4 1.5 copy-done.2
  171.8 4.9 %multiply_convert_fusion.5 = (bf16[512,768]{1,0:T(8,128)(2,1)S(1)}, bf16[512,768]{1,0:T(8,128)(2,1)S(1)}) fusion(f32[512,1536]{1,0:T(8,128)S(1)} %copy-done.2, bf16[512,2048]{1,0:T(8,128)(2,1)S(1)} %bitcast.123, bf16[1,768,2048]{2,1,0:T(8,128)(2,1)} %all-gather.3.cloned.1.call-done), kind=kOutput, calls=%fused_computation.46 | convolution fusion | flops 1616117760 | bytes 9961472 | tf_op jit(solution)/shard_map/dot_general | solution.py:33
  176.8 5.7 %fusion = bf16[1,2048,1536]{2,1,0:T(8,128)(2,1)} fusion(bf16[512,2048]{1,0:T(8,128)(2,1)S(1)} %bitcast.121, bf16[512,768]{1,0:T(8,128)(2,1)S(1)} %get-tuple-element.26, bf16[512,768]{1,0:T(8,128)(2,1)S(1)} %get-tuple-element.25), kind=kOutput, calls=%fused_computation.3 | convolution fusion | flops 3230662656 | bytes 9961472 | tf_op jit(solution)/shard_map/dot_general | solution.py:165
  182.5 7.6 %multiply_convert_fusion.2 = bf16[512,2048]{1,0:T(8,128)(2,1)} fusion(bf16[1,2048,1536]{2,1,0:T(8,128)(2,1)} %all-gather.5.cloned.1.call-done, bf16[512,768]{1,0:T(8,128)(2,1)S(1)} %get-tuple-element.26, bf16[512,768]{1,0:T(8,128)(2,1)S(1)} %get-tuple-element.25), kind=kOutput, calls=%fused_computation.21 | convolution fusion | flops 3226468352 | bytes 9961472 | tf_op jit(solution)/shard_map/dot_general | solution.py:46
  190.0 4.0 %all-to-all-start.3 = ((bf16[16,32,2048]{2,1,0:T(8,128)(2,1)}), bf16[16,32,2048]{2,1,0:T(8,128)(2,1)S(1)}, u32[]{:S(2)}, u32[]{:S(2)}) async-start(bf16[16,32,2048]{2,1,0:T(8,128)(2,1)} %bitcast.122), calls=%async_computation.3 | async-start | bytes 4194304 | tf_op jit(solution)/shard_map/all_to_all | solution.py:181
  194.6 0.1 copy.74
  194.7 0.1 copy.73
  194.8 0.6 pad_maximum_fusion.6
  195.4 39.4 %all-to-all-done.3 = bf16[16,32,2048]{2,1,0:T(8,128)(2,1)S(1)} async-done(((bf16[16,32,2048]{2,1,0:T(8,128)(2,1)}), bf16[16,32,2048]{2,1,0:T(8,128)(2,1)S(1)}, u32[]{:S(2)}, u32[]{:S(2)}) %all-to-all-start.3) | async-done | bytes 2097184 | tf_op jit(solution)/shard_map/all_to_all | solution.py:181
  234.8 0.1 fusion.45
  234.9 0.2 fusion.22
  235.2 0.3 fusion.21
  235.4 0.7 pad_maximum_fusion.5
  236.2 7.3 %select_convert_fusion.3 = (bf16[1,384,2048]{2,1,0:T(8,128)(2,1)}, bf16[1,384,2048]{2,1,0:T(8,128)(2,1)}, bf16[1,384,2048]{2,1,0:T(8,128)(2,1)}) fusion(bf16[1,384,2048]{2,1,0:T(8,128)(2,1)} %reduce-scatter.5.cloned.1.call-done, bf16[1,384,2048]{2,1,0:T(8,128)(2,1)} %param.23, pred[]{:T(512)} %bitcast.29, bf16[1,384,2048]{2,1,0:T(8,128)(2,1)} %param.25, ...), kind=kLoop, calls=%fused_computation.29 | loop fusion | flops 18087936 | bytes 12582913 | tf_op jit(solution)/shard_map/convert_element_type | solution.py:66
  243.5 45.4 %reduce-scatter.3.cloned.1.call-done = bf16[1,1024,1536]{2,1,0:T(8,128)(2,1)} async-done(((bf16[1,2048,1536]{2,1,0:T(8,128)(2,1)}), bf16[1,1024,1536]{2,1,0:T(8,128)(2,1)}) %reduce-scatter.3.cloned.1.call-update) | async-done | bytes 3145744 | tf_op jit(solution)/shard_map/reduce_scatter | solution.py:172
  288.9 13.1 %select_convert_fusion = (bf16[1,1024,1536]{2,1,0:T(8,128)(2,1)}, bf16[1,1024,1536]{2,1,0:T(8,128)(2,1)}, bf16[1,1024,1536]{2,1,0:T(8,128)(2,1)}) fusion(bf16[1,1024,1536]{2,1,0:T(8,128)(2,1)} %reduce-scatter.3.cloned.1.call-done, bf16[1,1024,1536]{2,1,0:T(8,128)(2,1)} %param.21, pred[]{:T(512)} %bitcast.29, bf16[1,1024,1536]{2,1,0:T(8,128)(2,1)} %param.24, ...), kind=kLoop, calls=%fused_computation.10 | loop fusion | flops 36175872 | bytes 25165824 | tf_op jit(solution)/shard_map/convert_element_type | solution.py:66
  (44 shorter events, 0.7 us)
Async XLA Ops:
  7.2 0.8 copy-start.7
  7.2 3.5 %copy-start.5 = (bf16[2,24,2048]{2,1,0:T(8,128)(2,1)S(1)}, bf16[2,24,2048]{2,1,0:T(8,128)(2,1)}, u32[]{:S(2)}) copy-start(bf16[2,24,2048]{2,1,0:T(8,128)(2,1)} %param.13) | copy-start | bytes 589828
  7.2 85.5 %all-gather.5.cloned.1.call-start = ((), (), s32[]{:S(2)}) async-start(), calls=%async_computation.8 | async-start | bytes 9437184 | tf_op jit(solution)/shard_map/all_gather | solution.py:114
  11.6 9.0 %copy-start.6 = (bf16[2,24,2048]{2,1,0:T(8,128)(2,1)S(1)}, bf16[2,24,2048]{2,1,0:T(8,128)(2,1)}, u32[]{:S(2)}) copy-start(bf16[2,24,2048]{2,1,0:T(8,128)(2,1)} %param.14) | copy-start | bytes 589828
  13.2 48.5 %all-to-all-start.2 = ((bf16[16,32,2048]{2,1,0:T(8,128)(2,1)}), bf16[16,32,2048]{2,1,0:T(8,128)(2,1)S(1)}, u32[]{:S(2)}, u32[]{:S(2)}) async-start(bf16[16,32,2048]{2,1,0:T(8,128)(2,1)} %pad_maximum_fusion.1), calls=%async_computation.2 | async-start | bytes 4194304 | tf_op jit(solution)/shard_map/all_to_all | solution.py:140
  61.7 1.3 copy-start.3
  63.0 76.2 %all-to-all-start.1 = ((bf16[16,32,2048]{2,1,0:T(8,128)(2,1)}), bf16[16,32,2048]{2,1,0:T(8,128)(2,1)S(1)}, u32[]{:S(2)}, u32[]{:S(2)}) async-start(bf16[16,32,2048]{2,1,0:T(8,128)(2,1)} %pad_maximum_fusion), calls=%async_computation.1 | async-start | bytes 4194304 | tf_op jit(solution)/shard_map/all_to_all | solution.py:141
  74.2 65.0 %all-gather.3.cloned.1.call-start = ((), (), s32[]{:S(2)}) async-start(), calls=%async_computation.7 | async-start | bytes 4718592 | tf_op jit(solution)/shard_map/all_gather | solution.py:115
  98.9 1.7 copy-start.1
  101.0 48.4 %copy-start.8 = (bf16[2,24,8]{1,2,0:T(8,128)(2,1)S(1)}, bf16[2,24,8]{1,2,0:T(8,128)(2,1)}, u32[]{:S(2)}) copy-start(bf16[2,24,8]{1,2,0:T(8,128)(2,1)} %param.16) | copy-start | bytes 2308
  143.7 12.0 %all-to-all-start.4 = ((bf16[16,1,32]{2,1,0:T(2,128)(2,1)}), bf16[16,1,32]{2,1,0:T(2,128)(2,1)S(1)}, u32[]{:S(2)}, u32[]{:S(2)}) async-start(bf16[16,1,32]{2,1,0:T(2,128)(2,1)} %convert_element_type.264), calls=%async_computation.4 | async-start | bytes 16384 | tf_op jit(solution)/shard_map/all_to_all | solution.py:188
  149.4 86.8 %reduce-scatter.5.cloned.1.call-start = ((), (), s32[]{:S(2)}) async-start(), calls=%async_computation.10 | async-start | bytes 4718592 | tf_op jit(solution)/shard_map/reduce_scatter | solution.py:175
  169.7 119.2 %reduce-scatter.3.cloned.1.call-start = ((), (), s32[]{:S(2)}) async-start(), calls=%async_computation.9 | async-start | bytes 9437184 | tf_op jit(solution)/shard_map/reduce_scatter | solution.py:172
  169.9 1.9 copy-start.2
  171.8 4.9 %copy-start.4 = (bf16[16,32,2048]{2,1,0:T(8,128)(2,1)S(1)}, bf16[16,32,2048]{2,1,0:T(8,128)(2,1)}, u32[]{:S(2)}) copy-start(bf16[16,32,2048]{2,1,0:T(8,128)(2,1)} %copy-done.3) | copy-start | bytes 6291460
  190.0 44.8 %all-to-all-start.3 = ((bf16[16,32,2048]{2,1,0:T(8,128)(2,1)}), bf16[16,32,2048]{2,1,0:T(8,128)(2,1)S(1)}, u32[]{:S(2)}, u32[]{:S(2)}) async-start(bf16[16,32,2048]{2,1,0:T(8,128)(2,1)} %bitcast.122), calls=%async_computation.3 | async-start | bytes 4194304 | tf_op jit(solution)/shard_map/all_to_all | solution.py:181
  236.2 52.7 %copy-start = (bf16[1,1024,1536]{2,1,0:T(8,128)(2,1)S(1)}, bf16[1,1024,1536]{2,1,0:T(8,128)(2,1)}, u32[]{:S(2)}) copy-start(bf16[1,1024,1536]{2,1,0:T(8,128)(2,1)} %param.18) | copy-start | bytes 9437188
Sparse Core Ops, SparseCore 0:
  9.6 83.1 all-gather.4
  94.3 44.9 all-gather.2
  169.8 39.6 reduce-scatter.4
  211.8 77.0 reduce-scatter.2
where the time goes:
time: 309 us
  waiting for transfers between devices  187 us (61%)
  matrix products  34 us (11%)
  other arithmetic  28.6 us (9%)
  starting transfers between devices  28.5 us (9%)
  between operations  14.7 us (5%)
  blocking collectives  8.98 us (3%)
  local copies, waits for them, and re-layouts  6.97 us (2%)
    reduce_scatter x1, waiting for transfers between devices, body(): lax.psum_scatter(grad_in[None].astype(jnp.bfloat16), 'rep', scatter_dimen...  45.4 us
    all_to_all x1, waiting for transfers between devices, body(): lax.all_to_all(rows_dx.reshape(sources, -1, model_width), 'exp', split_ax...  39.4 us
    all_to_all x1, waiting for transfers between devices, body(): lax.all_to_all(joined[0], 'exp', split_axis=0, concat_axis=0, tiled=True)  38.6 us
    all_gather x1, waiting for transfers between devices, body(): lax.all_gather(w_out, 'rep', axis=1, tiled=True)  38.2 us
    convert_element_type x2, other arithmetic, adam_update(): jnp.where(alive_mask, second_new, jnp.zeros_like(second_new))  20.4 us
    all_gather x1, waiting for transfers between devices, body(): lax.all_gather(w_in, 'rep', axis=1, tiled=True)  17.7 us
    all_to_all x1, starting transfers between devices, body(): lax.all_to_all(joined[1], 'exp', split_axis=0, concat_axis=0, tiled=True)  11.2 us
    all_to_all x1, blocking collectives, body(): lax.all_to_all(joined[2], 'exp', split_axis=0, concat_axis=0, tiled=True)  8.98 us
  transfers between devices with their start and end apart: 8, of which 6 were waited for; matrix products, arithmetic and copies ran while one was open for 14% of the time, Pallas kernels for 0%

commit v1 on v0

--- a/solution.py
+++ b/solution.py
@@ -231,7 +231,126 @@
     )
 
 
+def partial_body(
+    tokens,
+    cotangent,
+    routes,
+    gates,
+    collapsed,
+    w_in,
+    w_out,
+    first_in,
+    second_in,
+    first_out,
+    second_out,
+    fresh_in,
+    fresh_out,
+):
+    micro, rows, width = tokens.shape
+    replicas = lax.axis_size("rep")
+    sources = lax.axis_size("exp")
+    devices = replicas * sources
+    num_exp = sources
+    hidden = w_in.shape[2] // 2
+    part = hidden // replicas
+    me_rep = lax.axis_index("rep")
+    me_exp = lax.axis_index("exp")
+    scale_in = 1.0 / math.sqrt(width)
+    scale_out = 1.0 / math.sqrt(hidden)
+    both = ("rep", "exp")
+    swap = [(0, 1), (1, 0)]
+    depth = w_in.shape[1]
+
+    columns = w_in[0].reshape(depth, 2, replicas, part)
+    mine = lax.dynamic_index_in_dim(columns, me_rep, 2, keepdims=False).reshape(depth, 2 * part)
+    theirs = lax.dynamic_index_in_dim(columns, 1 - me_rep, 2, keepdims=False).reshape(
+        depth, 2 * part
+    )
+    got = lax.ppermute(theirs, "rep", swap)
+    low = me_rep == 0
+    weight_in = jnp.concatenate([jnp.where(low, mine, got), jnp.where(low, got, mine)], axis=0)
+    weight_out = w_out[0]
+
+    chosen = routes[..., None] == jnp.arange(num_exp, dtype=jnp.int32)
+    spread = jnp.sum(jnp.where(chosen, gates[..., None], 0).astype(jnp.float32), axis=2)
+    all_gates = lax.all_gather(spread.astype(jnp.bfloat16), both, axis=0)
+    all_tokens = lax.all_gather(tokens, both, axis=0).reshape(-1, width)
+    all_cots = lax.all_gather(cotangent, both, axis=0).reshape(-1, width)
+    is_me = jnp.arange(num_exp, dtype=jnp.int32) == me_exp
+    gate = jnp.sum(
+        jnp.where(is_me, all_gates.reshape(-1, num_exp).astype(jnp.float32), 0.0),
+        axis=1,
+        keepdims=True,
+    )
+
+    pre = jnp.dot(all_tokens, weight_in, preferred_element_type=jnp.float32) * scale_in
+    half, up = pre[:, :part], pre[:, part:]
+    silu_val, slope = silu_parts(half)
+    active = (silu_val * up).astype(jnp.bfloat16)
+    back = (
+        lax.dot_general(
+            all_cots, weight_out, (((1,), (1,)), ((), ())), preferred_element_type=jnp.float32
+        )
+        * scale_out
+    )
+    gate_grad = jnp.sum(active.astype(jnp.float32) * back, axis=1)
+    act_cot = back * gate
+    pre_cot = jnp.concatenate([act_cot * up * slope, act_cot * silu_val], axis=1).astype(
+        jnp.bfloat16
+    )
+    gated = (active.astype(jnp.float32) * gate).astype(jnp.bfloat16)
+    grad_in = (
+        lax.dot_general(
+            all_tokens, pre_cot, (((0,), (0,)), ((), ())), preferred_element_type=jnp.float32
+        )
+        * scale_in
+    ).astype(jnp.bfloat16)
+    sides = grad_in.reshape(replicas, depth, 2 * part)
+    own_side = lax.dynamic_index_in_dim(sides, me_rep, 0, keepdims=False)
+    far_side = lax.dynamic_index_in_dim(sides, 1 - me_rep, 0, keepdims=False)
+    came = lax.ppermute(far_side, "rep", swap)
+    rows_dx = (
+        lax.dot_general(
+            pre_cot, weight_in, (((1,), (1,)), ((), ())), preferred_element_type=jnp.float32
+        )
+        * scale_in
+    ).astype(jnp.bfloat16)
+    token_dx = lax.psum_scatter(
+        rows_dx.reshape(devices, micro, rows, width), both, scatter_dimension=0, tiled=False
+    )
+    dense = jnp.where(is_me, gate_grad[:, None], 0.0).reshape(devices, micro * rows * num_exp)
+    token_gate = lax.psum_scatter(dense, both, scatter_dimension=0, tiled=False)
+    token_gate = token_gate.reshape(micro, rows, 1, num_exp)
+    d_gates = jnp.sum(jnp.where(chosen, token_gate, 0.0), axis=3).astype(jnp.bfloat16)
+    grad_out = (
+        lax.dot_general(
+            gated, all_cots, (((0,), (0,)), ((), ())), preferred_element_type=jnp.float32
+        )
+        * scale_out
+    )[None]
+    first_cols = jnp.where(low, own_side, came)
+    last_cols = jnp.where(low, came, own_side)
+    full_grad = jnp.concatenate(
+        [first_cols[:, :part], last_cols[:, :part], first_cols[:, part:], last_cols[:, part:]],
+        axis=1,
+    )[None].astype(jnp.float32)
+    dead_flag = collapsed.reshape(-1, 1, 1)
+    updated_in = adam_update(w_in, first_in, second_in, full_grad, fresh_in, dead_flag)
+    updated_out = adam_update(w_out, first_out, second_out, grad_out, fresh_out, dead_flag)
+    return (
+        token_dx,
+        d_gates,
+        updated_in[0],
+        updated_out[0],
+        updated_in[1],
+        updated_in[2],
+        updated_out[1],
+        updated_out[2],
+    )
+
+
 def solution(mesh):
+    inner = partial_body if mesh.shape["rep"] == 2 else body
     placed = (
         P(None, ("rep", "exp"), None),
         P(None, ("rep", "exp"), None),
@@ -248,7 +367,7 @@
         P("exp", "rep", None),
     )
     return jax.shard_map(
-        body,
+        inner,
         mesh=mesh,
         in_specs=placed,
         out_specs=(

time: 309 us -> 439 us (1.42); the launches traced: 309 us -> 431 us
  local copies, waits for them, and re-layouts: 6.97 us -> 64.6 us
  waiting for transfers between devices: 187 us -> 240 us
  blocking collectives: 8.98 us -> 43.1 us
  starting transfers between devices: 28.5 us -> 4.89 us
  matrix products: 34 us -> 51.6 us
  other arithmetic: 28.6 us -> 12 us
    all_to_all x4 -> x0, waiting for transfers between devices: 84.1 us -> none  [the longest x1 39.4 us: body(): lax.all_to_all(rows_dx.reshape(sources, -1, model_width), 'exp', split_ax...]
    unnamed x4 -> x5, waiting for transfers between devices: 1.41 us -> 64.1 us
    reduce_scatter x2 -> x1, waiting for transfers between devices: 45.4 us -> 105 us  [partial_body(): lax.psum_scatter(rows_dx.reshape(devices, micro, rows, width), both, scat...]
    dynamic_slice x0 -> x4, local copies, waits for them, and re-layouts: none -> 45.6 us  [the longest x1 22.5 us: partial_body(): lax.dynamic_index_in_dim(columns, me_rep, 2, keepdims=False)]
    all_gather x0 -> x1, blocking collectives: none -> 43.1 us  [partial_body(): all_gates = lax.all_gather(spread.astype(jnp.bfloat16), both, axis=0)]
    all_to_all x4 -> x0, starting transfers between devices: 28.1 us -> none  [the longest x1 11.2 us: body(): lax.all_to_all(joined[1], 'exp', split_axis=0, concat_axis=0, tiled=True)]
    dot_general x12 -> x5, matrix products: 34 us -> 51.6 us  [the longest x1 12.4 us: partial_body(): lax.dot_general(gated, all_cots, (((0,), (0,)), ((), ())), preferred_elem...]
    convert_element_type x2 -> x1, other arithmetic: 20.4 us -> 8.3 us  [adam_update(): jnp.where(alive_mask, second_new, jnp.zeros_like(second_new))]
  transfers between devices with their start and end apart: 8 -> 6, of which waited for: 6 -> 5; matrix products, arithmetic and copies ran while one was open for 14% -> 26% of each run, Pallas kernels for 0% -> 0%
where the time goes in v1:
time: 439 us; the launch traced here: 431 us
  waiting for transfers between devices  240 us (55%)
  local copies, waits for them, and re-layouts  64.6 us (15%)
  matrix products  51.6 us (12%)
  blocking collectives  43.1 us (10%)
  between operations  15 us (3%)
  other arithmetic  12 us (3%)
  starting transfers between devices  4.89 us (1%)
    reduce_scatter x1, waiting for transfers between devices, partial_body(): lax.psum_scatter(rows_dx.reshape(devices, micro, rows, width), both, scat...  105 us
    unnamed x5, waiting for transfers between devices  64.1 us
    all_gather x1, waiting for transfers between devices, partial_body(): all_cots = lax.all_gather(cotangent, both, axis=0).reshape(-1, width)  62 us
    all_gather x1, blocking collectives, partial_body(): all_gates = lax.all_gather(spread.astype(jnp.bfloat16), both, axis=0)  43.1 us
    dynamic_slice x1, local copies, waits for them, and re-layouts, partial_body(): lax.dynamic_index_in_dim(columns, me_rep, 2, keepdims=False)  22.5 us
    dynamic_slice x2, local copies, waits for them, and re-layouts, partial_body(): own_side = lax.dynamic_index_in_dim(sides, me_rep, 0, keepdims=False)  17.5 us
    dot_general x1, matrix products, partial_body(): lax.dot_general(gated, all_cots, (((0,), (0,)), ((), ())), preferred_elem...  12.4 us
    dot_general x1, matrix products, partial_body(): lax.dot_general(all_cots, weight_out, (((1,), (1,)), ((), ())), preferred...  10.1 us
  transfers between devices with their start and end apart: 6, of which 5 were waited for; matrix products, arithmetic and copies ran while one was open for 26% of the time, Pallas kernels for 0%

profile of v1, /device:TPU:0, one launch (start us, length us, event | category | flops | bytes accessed | tf_op | source)
XLA Modules:
  0.0 431.3 jit_solution(11811751298307628185)
XLA Ops:
  7.2 0.0 all-gather.8.cloned.1.call-start
  7.2 0.7 all-gather.8.cloned.1.call-update
  7.9 0.0 all-gather.6.cloned.1.call-start
  7.9 0.7 all-gather.6.cloned.1.call-update
  8.6 0.0 all-reduce.3.cloned.1.call-start
  8.7 6.2 %reshape_squeeze.3 = bf16[1024,2,2,384]{3,2,1,0:T(2,128)(2,1)S(1)} reshape(bf16[1,1024,1536]{2,1,0:T(8,128)(2,1)} %param.18) | data formatting | bytes 6291456 | tf_op jit(solution)/shard_map/reshape;squeeze | solution.py:264
  14.9 22.5 %dynamic-slice_reduce_fusion.1 = (bf16[1024,2,384]{2,1,0:T(2,128)(2,1)}, bf16[1024,2,384]{2,1,0:T(2,128)(2,1)S(1)}) fusion(bf16[1024,2,2,384]{3,2,1,0:T(2,128)(2,1)S(1)} %reshape_squeeze.3, s32[]{:T(128)S(6)} %select_n.71, s32[]{:T(128)S(6)} %select_n.72), kind=kLoop, calls=%fused_computation.18 | loop fusion | bytes 6291464 | tf_op jit(solution)/shard_map/jit(dynamic_index_in_dim)/dynamic_slice | solution.py:265
  37.4 0.0 copy-start.7
  37.4 0.0 copy-start.8
  37.4 0.0 copy-start.2
  37.4 0.3 copy.58
  37.8 3.0 collective-permute-start
  40.8 0.1 broadcast_in_dim.100
  40.9 0.0 copy-done.7
  40.9 0.0 copy-done.8
  40.9 43.1 %all-gather.1 = bf16[64,24,16]{1,2,0:T(8,128)(2,1)S(1)} all-gather(bf16[2,24,16]{1,2,0:T(8,128)(2,1)S(1)} %fusion.13), channel_id=3, replica_groups=mesh['rep'=2,'exp'=16] {'rep','exp'}, dimensions={0}, use_global_device_ids=true | all-gather | bytes 50688 | tf_op jit(solution)/shard_map/all_gather | solution.py:276
  84.1 0.2 fusion.11
  84.3 0.1 mul.177
  84.4 0.0 copy-done.2
  84.4 0.3 copy.57
  84.7 5.9 %collective-permute-done = bf16[1024,768]{1,0:T(8,128)(2,1)} collective-permute-done((bf16[1024,768]{1,0:T(8,128)(2,1)S(1)}, bf16[1024,768]{1,0:T(8,128)(2,1)}, u32[]{:S(2)}, u32[]{:S(2)}) %collective-permute-start) | collective-permute-done | bytes 1572896 | tf_op jit(solution)/shard_map/ppermute | solution.py:269
  90.7 1.6 broadcast_select_fusion.1
  92.3 2.9 all-gather.8.cloned.1.call-done
  95.2 9.6 %multiply_bitcast_fusion = f32[1536,768]{0,1:T(8,128)} fusion(bf16[1536,2048]{1,0:T(8,128)(2,1)} %bitcast.63, bf16[1024,768]{1,0:T(8,128)(2,1)S(1)} %get-tuple-element.27, bf16[1024,768]{1,0:T(8,128)(2,1)S(1)} %get-tuple-element.26), kind=kOutput, calls=%fused_computation.9 | convolution fusion | flops 4839309312 | bytes 14155776 | tf_op jit(solution)/shard_map/dot_general | solution.py:286
  104.8 62.0 %all-gather.6.cloned.1.call-done = bf16[64,24,2048]{2,1,0:T(8,128)(2,1)} async-done(((bf16[2,24,2048]{2,1,0:T(8,128)(2,1)}), bf16[64,24,2048]{2,1,0:T(8,128)(2,1)}) %all-gather.6.cloned.1.call-update) | async-done | bytes 6291472 | tf_op jit(solution)/shard_map/all_gather | solution.py:278
  166.8 10.1 %fusion.3 = (f32[1536]{0:T(1024)S(1)}, bf16[1536,384]{0,1:T(8,128)(2,1)}, bf16[1536,384]{0,1:T(8,128)(2,1)}, bf16[1536,384]{0,1:T(8,128)(2,1)}) fusion(f32[1536,768]{0,1:T(8,128)} %multiply_bitcast_fusion, f32[1536]{0:T(1024)S(1)} %broadcast_multiply_fusion, bf16[1536,2048]{1,0:T(8,128)(2,1)} %bitcast.61, bf16[1,384,2048]{2,1,0:T(8,128)(2,1)} %param.19), kind=kOutput, calls=%fused_computation.22 | convolution fusion | flops 2427714048 | bytes 16134144 | tf_op jit(solution)/shard_map/dot_general | solution.py:291
  176.9 0.1 broadcast_in_dim.102
  177.0 0.1 copy.49
  177.1 0.9 bitcast_select_fusion.2
  178.0 0.0 all-reduce.3.cloned.1.call-update
  178.0 0.2 reduce-scatter.3.cloned.1.call-start
  178.3 9.8 %multiply_convert_fusion = bf16[1536,2048]{1,0:T(8,128)(2,1)} fusion(bf16[1024,768]{1,0:T(8,128)(2,1)S(1)} %get-tuple-element.27, bf16[1024,768]{1,0:T(8,128)(2,1)S(1)} %get-tuple-element.26, bf16[1536,384]{0,1:T(8,128)(2,1)} %get-tuple-element.14, bf16[1536,384]{0,1:T(8,128)(2,1)} %get-tuple-element.15), kind=kOutput, calls=%fused_computation | convolution fusion | flops 4849139712 | bytes 11796480 | tf_op jit(solution)/shard_map/dot_general | solution.py:313
  188.0 0.0 copy-start.9
  188.0 0.0 copy-start.10
  188.0 0.0 reduce-scatter.3.cloned.1.call-update
  188.9 0.5 copy-done.9
  189.3 0.4 copy-done.10
  189.7 9.7 %fusion.2 = bf16[2048,768]{0,1:T(8,128)(2,1)} fusion(bf16[1536,2048]{1,0:T(8,128)(2,1)} %bitcast.64, bf16[1536,384]{0,1:T(8,128)(2,1)S(1)} %copy-done.9, bf16[1536,384]{0,1:T(8,128)(2,1)S(1)} %copy-done.10), kind=kOutput, calls=%fused_computation.19 | convolution fusion | flops 4839702528 | bytes 11796480 | tf_op jit(solution)/shard_map/dot_general | solution.py:303
  199.4 5.0 %reshape.153 = bf16[2,1024,768]{1,0,2:T(2,128)(2,1)S(1)} reshape(bf16[2048,768]{0,1:T(8,128)(2,1)} %fusion.2) | data formatting | bytes 6291456 | tf_op jit(solution)/shard_map/reshape | solution.py:308
  204.4 9.2 %constant_dynamic-slice_fusion.1 = (bf16[1,1024,768]{1,0,2:T(2,128)(2,1)}, bf16[1,1024,768]{1,0,2:T(2,128)(2,1)}) fusion(bf16[2,1024,768]{1,0,2:T(2,128)(2,1)S(1)} %reshape.153, s32[]{:T(128)S(6)} %select_n.71, s32[]{:T(128)S(6)} %select_n.72), kind=kLoop, calls=%fused_computation.52 | loop fusion | bytes 6291464 | tf_op jit(solution)/shard_map/jit(dynamic_index_in_dim)/dynamic_slice | solution.py:309
  213.6 0.0 copy-start
  213.6 8.3 %copy.51 = bf16[1,1024,768]{2,1,0:T(8,128)(2,1)} copy(bf16[1,1024,768]{1,0,2:T(2,128)(2,1)} %get-tuple-element.24) | data formatting | bytes 3145728 | tf_op jit(solution)/shard_map/jit(dynamic_index_in_dim)/dynamic_slice | solution.py:309
  221.9 0.0 copy-done
  221.9 5.7 %copy.52 = bf16[1,1024,768]{2,1,0:T(8,128)(2,1)} copy(bf16[1,1024,768]{1,0,2:T(2,128)(2,1)S(1)} %copy-done) | data formatting | bytes 3145728 | tf_op jit(solution)/shard_map/jit(dynamic_index_in_dim)/dynamic_slice | solution.py:310
  227.5 1.5 collective-permute-start.1
  229.1 0.0 copy-start.3
  229.1 12.4 %select_convert_fusion.3 = (bf16[1,384,2048]{2,1,0:T(8,128)(2,1)}, bf16[1,384,2048]{2,1,0:T(8,128)(2,1)}, bf16[1,384,2048]{2,1,0:T(8,128)(2,1)}) fusion(bf16[1,384,2048]{2,1,0:T(8,128)(2,1)} %param.23, pred[]{:T(512)} %bitcast.8, bf16[1,384,2048]{2,1,0:T(8,128)(2,1)} %param.25, bf16[1,384,2048]{2,1,0:T(8,128)(2,1)} %param.22, ...), kind=kOutput, calls=%fused_computation.14 | convolution fusion | flops 2435776512 | bytes 18487296 | tf_op jit(solution)/shard_map/dot_general | solution.py:326
  241.5 62.7 %all-reduce.3.cloned.1.call-done = f32[32,768]{0,1:T(8,128)} async-done(((f32[32,768]{0,1:T(8,128)}), f32[32,768]{0,1:T(8,128)}) %all-reduce.3.cloned.1.call-update) | async-done | bytes 98320
  304.2 1.3 dynamic-slice_reduce_fusion.2
  305.5 0.1 broadcast_in_dim.106
  305.5 0.1 copy.50
  305.6 0.6 select_reduce_fusion
  306.3 0.0 collective-permute-done.1
  306.3 0.0 copy-done.3
  306.3 0.2 bitcast_select_fusion.1
  306.5 0.0 copy-start.1
  306.5 0.0 copy-start.4
  306.5 0.3 slice_bitcast_fusion.2
  306.8 1.3 copy-done.5
  308.2 1.0 copy-done.6
  309.1 1.0 copy-done.1
  310.1 0.9 copy-done.4
  311.0 8.3 %select_convert_fusion = (bf16[1,1024,1536]{2,1,0:T(8,128)(2,1)}, bf16[1,1024,1536]{2,1,0:T(8,128)(2,1)}, bf16[1,1024,1536]{2,1,0:T(8,128)(2,1)}) fusion(bf16[1,1024,1536]{2,1,0:T(8,128)(2,1)S(1)} %copy-done.4, pred[]{:T(512)} %bitcast.8, bf16[1,1024,384]{2,1,0:T(8,128)(2,1)S(1)} %get-tuple-element.31, bf16[1,1024,384]{2,1,0:T(8,128)(2,1)S(1)} %get-tuple-element.32, ...), kind=kLoop, calls=%fused_computation.5 | loop fusion | flops 47185920 | bytes 25165824 | tf_op jit(solution)/shard_map/convert_element_type | solution.py:66
  319.3 105.2 %reduce-scatter.3.cloned.1.call-done = bf16[1,2,24,2048]{3,2,1,0:T(8,128)(2,1)} async-done(((bf16[32,2,24,2048]{3,2,1,0:T(8,128)(2,1)}), bf16[1,2,24,2048]{3,2,1,0:T(8,128)(2,1)}) %reduce-scatter.3.cloned.1.call-update) | async-done | bytes 196624 | tf_op jit(solution)/shard_map/reduce_scatter | solution.py:318
  (6 shorter events, 0.0 us)
Async XLA Ops:
  7.2 88.0 %all-gather.8.cloned.1.call-start = ((), (), s32[]{:S(2)}) async-start(), calls=%async_computation.3 | async-start | bytes 6488064 | tf_op jit(solution)/shard_map/all_gather | solution.py:277
  7.9 158.9 %all-gather.6.cloned.1.call-start = ((), (), s32[]{:S(2)}) async-start(), calls=%async_computation.2 | async-start | bytes 6488064 | tf_op jit(solution)/shard_map/all_gather | solution.py:278
  8.6 295.5 %all-reduce.3.cloned.1.call-start = ((), (), s32[]{:S(2)}) async-start(), calls=%async_computation.4 | async-start | bytes 786432
  37.4 3.5 copy-start.7
  37.4 3.5 copy-start.8
  37.4 46.9 %copy-start.2 = (bf16[1024,2,384]{2,1,0:T(2,128)(2,1)S(1)}, bf16[1024,2,384]{2,1,0:T(2,128)(2,1)}, u32[]{:S(2)}) copy-start(bf16[1024,2,384]{2,1,0:T(2,128)(2,1)} %get-tuple-element.8) | copy-start | bytes 4718596
  37.8 52.9 %collective-permute-start = (bf16[1024,768]{1,0:T(8,128)(2,1)S(1)}, bf16[1024,768]{1,0:T(8,128)(2,1)}, u32[]{:S(2)}, u32[]{:S(2)}) collective-permute-start(bf16[1024,768]{1,0:T(8,128)(2,1)S(1)} %bitcast.58), channel_id=1, source_target_pairs={{0,16},{16,0},{1,17},{17,1},{2,18},{18,2},{3,19},{19,3},{4,20},{20... | collective-permute-start | bytes 4718600 | tf_op jit(solution)/shard_map/ppermute | solution.py:269
  178.0 246.4 %reduce-scatter.3.cloned.1.call-start = ((), (), s32[]{:S(2)}) async-start(), calls=%async_computation.1 | async-start | bytes 6488064 | tf_op jit(solution)/shard_map/reduce_scatter | solution.py:318
  188.0 1.3 copy-start.9
  188.0 1.6 copy-start.10
  213.6 8.3 %copy-start = (bf16[1,1024,768]{1,0,2:T(2,128)(2,1)S(1)}, bf16[1,1024,768]{1,0,2:T(2,128)(2,1)}, u32[]{:S(2)}) copy-start(bf16[1,1024,768]{1,0,2:T(2,128)(2,1)} %get-tuple-element.25) | copy-start | bytes 4718596
  227.5 78.7 %collective-permute-start.1 = (bf16[1024,768]{1,0:T(8,128)(2,1)}, bf16[1024,768]{1,0:T(8,128)(2,1)S(1)}, u32[]{:S(2)}, u32[]{:S(2)}) collective-permute-start(bf16[1024,768]{1,0:T(8,128)(2,1)} %bitcast.59), channel_id=1, source_target_pairs={{0,16},{16,0},{1,17},{17,1},{2,18},{18,2},{3,19},{19,3},{4,20},{20... | collective-permute-start | bytes 4718600 | tf_op jit(solution)/shard_map/ppermute | solution.py:311
  229.1 77.2 %copy-start.3 = (bf16[1,1024,768]{2,1,0:T(8,128)(2,1)S(1)}, bf16[1,1024,768]{2,1,0:T(8,128)(2,1)}, u32[]{:S(2)}) copy-start(bf16[1,1024,768]{2,1,0:T(8,128)(2,1)} %copy.51) | copy-start | bytes 4718596
  306.3 1.9 copy-start.5
  306.3 2.8 copy-start.6
  306.5 3.6 copy-start.1
  306.5 4.5 %copy-start.4 = (bf16[1,1024,1536]{2,1,0:T(8,128)(2,1)S(1)}, bf16[1,1024,1536]{2,1,0:T(8,128)(2,1)}, u32[]{:S(2)}) copy-start(bf16[1,1024,1536]{2,1,0:T(8,128)(2,1)} %param.21) | copy-start | bytes 9437188
Sparse Core Ops, SparseCore 0:
  10.9 84.2 all-gather.7
  98.1 68.7 all-gather.5
  178.2 125.9 all-reduce.2
  311.2 113.2 reduce-scatter.2

commit v2 on v1

--- a/solution.py
+++ b/solution.py
@@ -3,6 +3,8 @@
 import jax
 import jax.numpy as jnp
 from jax import lax
+from jax.experimental import pallas as pl
+from jax.experimental.pallas import tpu as pltpu
 from jax.sharding import PartitionSpec as P
 
 beta_one = 0.9
@@ -231,6 +233,344 @@
     )
 
 
+MESH = pl.DeviceIdType.MESH
+Z_SIDE = 4
+
+
+def where_am_i():
+    y = lax.axis_index("rep")
+    e = lax.axis_index("exp")
+    return y, e // 4, (e // 2) % 2, e % 2
+
+
+def place_of(here, dy, dz, dx, dc):
+    y, z, x, c = here
+    return (y + dy) % 2, ((z + dz) % Z_SIDE) * 4 + ((x + dx) % 2) * 2 + (c + dc) % 2
+
+
+def slot_of(here, dy, dz, dx, dc):
+    rep, exp = place_of(here, dy, dz, dx, dc)
+    return rep * 16 + exp
+
+
+def greet(here):
+    barrier = pltpu.get_barrier_semaphore()
+    near = [(1, 0, 0, 0), (0, 1, 0, 0), (0, 2, 0, 0), (0, 3, 0, 0), (0, 0, 1, 0), (0, 0, 0, 1)]
+    for step in near:
+        pl.semaphore_signal(barrier, inc=1, device_id=place_of(here, *step), device_id_type=MESH)
+    pl.semaphore_wait(barrier, len(near))
+
+
+def number_of(rel):
+    dy, dz, dx, dc = rel
+    return dy * 16 + dz * 4 + dx * 2 + dc
+
+
+def spread_kernel(
+    tok_ref, cot_ref, gate_ref, w_ref, tok_all, cot_all, gate_all, w_all, send, recv, local, w_send, w_recv
+):
+    here = where_am_i()
+    y = here[0]
+    own = (0, 0, 0, 0)
+    ins = (tok_ref, cot_ref, gate_ref)
+    outs = (tok_all, cot_all, gate_all)
+    depth = w_ref.shape[1]
+    part = w_all.shape[1] // 2
+
+    def copy(kind, rel, target, arrives):
+        slot = slot_of(here, *rel)
+        source = ins[kind] if rel == own else outs[kind].at[slot]
+        return pltpu.make_async_remote_copy(
+            src_ref=source,
+            dst_ref=outs[kind].at[slot],
+            send_sem=send.at[kind, number_of(arrives)],
+            recv_sem=recv.at[kind, number_of(arrives)],
+            device_id=place_of(here, *target),
+            device_id_type=MESH,
+        )
+
+    sent = []
+
+    def pass_on(rel, kinds=(0, 1, 2)):
+        dy, dz, dx, dc = rel
+        for kind in kinds:
+            goes = []
+            if dx == 0:
+                goes.append(((0, 0, 1, 0), (dy, dz, 1, 0)))
+            if dx == 0 and dy == 0:
+                goes.append(((1, 0, 0, 0), (1, dz, 0, 0)))
+            if rel == own:
+                for step in (1, 3, 2):
+                    goes.append(((0, Z_SIDE - step, 0, 0), (0, step, 0, 0)))
+            goes.append(((0, 0, 0, 1), (dy, dz, dx, 1)))
+            for target, arrives in goes:
+                one = copy(kind, rel, target, arrives)
+                one.start()
+                sent.append(one)
+
+    def landed(kind, rel):
+        slot = slot_of(here, *rel)
+        pltpu.make_async_remote_copy(
+            src_ref=outs[kind].at[slot],
+            dst_ref=outs[kind].at[slot],
+            send_sem=send.at[kind, number_of(rel)],
+            recv_sem=recv.at[kind, number_of(rel)],
+            device_id=place_of(here, 0, 0, 0, 1),
+            device_id_type=MESH,
+        ).wait_recv()
+
+    locals_ = []
+    for kind in range(3):
+        locals_.append(
+            pltpu.make_async_copy(ins[kind], outs[kind].at[slot_of(here, *own)], local.at[kind])
+        )
+    rows = pl.ds(pl.multiple_of(y * depth, depth), depth)
+    for side in range(2):
+        locals_.append(
+            pltpu.make_async_copy(
+                w_ref.at[0, :, pl.ds(pl.multiple_of(side * 2 * part + y * part, 128), part)],
+                w_all.at[rows, pl.ds(side * part, part)],
+                local.at[3 + side],
+            )
+        )
+    for one in locals_:
+        one.start()
+    greet(here)
+    pass_on(own)
+    swaps = []
+    for side in range(2):
+        swaps.append(
+            pltpu.make_async_remote_copy(
+                src_ref=w_ref.at[
+                    0, :, pl.ds(pl.multiple_of(side * 2 * part + (1 - y) * part, 128), part)
+                ],
+                dst_ref=w_all.at[rows, pl.ds(side * part, part)],
+                send_sem=w_send.at[side],
+                recv_sem=w_recv.at[side],
+                device_id=place_of(here, 1, 0, 0, 0),
+                device_id_type=MESH,
+            )
+        )
+        swaps[-1].start()
+    order = [(1, 0, 0, 0), (0, 1, 0, 0), (0, 3, 0, 0), (0, 0, 1, 0), (1, 1, 0, 0), (1, 3, 0, 0)]
+    order += [(0, 2, 0, 0), (1, 0, 1, 0), (1, 2, 0, 0)]
+    for dz in (1, 3, 2):
+        for dy in (0, 1):
+            order.append((dy, dz, 1, 0))
+    for rel in order:
+        for kind in range(3):
+            landed(kind, rel)
+            pass_on(rel, (kind,))
+    for dy in range(2):
+        for dz in range(Z_SIDE):
+            for dx in range(2):
+                for kind in range(3):
+                    landed(kind, (dy, dz, dx, 1))
+    for one in sent:
+        one.wait_send()
+    for one in swaps:
+        one.wait()
+    for one in locals_:
+        one.wait()
+
+
+def spread_all(tok, cot, gate, w_in):
+    rows, width = tok.shape
+    depth, columns = w_in.shape[1:]
+    whole = pl.BlockSpec(memory_space=pl.ANY)
+    return pl.pallas_call(
+        spread_kernel,
+        out_shape=(
+            jax.ShapeDtypeStruct((32, rows, width), jnp.bfloat16),
+            jax.ShapeDtypeStruct((32, rows, width), jnp.bfloat16),
+            jax.ShapeDtypeStruct((32,) + gate.shape, gate.dtype),
+            jax.ShapeDtypeStruct((2 * depth, columns // 2), jnp.bfloat16),
+        ),
+        in_specs=[whole] * 4,
+        out_specs=(whole,) * 4,
+        scratch_shapes=[
+            pltpu.SemaphoreType.DMA((3, 32)),
+            pltpu.SemaphoreType.DMA((3, 32)),
+            pltpu.SemaphoreType.DMA((5,)),
+            pltpu.SemaphoreType.DMA((2,)),
+            pltpu.SemaphoreType.DMA((2,)),
+        ],
+        compiler_params=pltpu.CompilerParams(collective_id=0, has_side_effects=True),
+        name="spread_all",
+    )(tok, cot, gate, w_in)
+
+
+def merge_kernel(
+    dx_ref,
+    dg_ref,
+    grad_ref,
+    dx_out,
+    dg_out,
+    grad_out,
+    r1x,
+    r2x,
+    r3x,
+    r4x,
+    s2x,
+    s3x,
+    s4x,
+    r1g,
+    r2g,
+    r3g,
+    r4g,
+    s2g,
+    s3g,
+    s4g,
+    send,
+    recv,
+    local,
+    g_send,
+    g_recv,
+):
+    here = where_am_i()
+    y = here[0]
+    depth = grad_out.shape[0]
+    part = grad_ref.shape[1] // 2
+    ins = (dx_ref, dg_ref)
+    stage_in = ((r1x, r2x, r3x, r4x), (r1g, r2g, r3g, r4g))
+    stage_out = ((None, s2x, s3x, s4x), (None, s2g, s3g, s4g))
+    firsts = (0, 16, 24, 28)
+
+    def copy(kind, stage, index, source, target):
+        return pltpu.make_async_remote_copy(
+            src_ref=source,
+            dst_ref=stage_in[kind][stage].at[index],
+            send_sem=send.at[kind, firsts[stage] + index],
+            recv_sem=recv.at[kind, firsts[stage] + index],
+            device_id=place_of(here, *target),
+            device_id_type=MESH,
+        )
+
+    sent = []
+
+    def go(kind, stage, index, source, target):
+        one = copy(kind, stage, index, source, target)
+        one.start()
+        sent.append(one)
+
+    def landed(kind, stage, index):
+        buffer = stage_in[kind][stage].at[index]
+        copy(kind, stage, index, buffer, (0, 0, 0, 1)).wait_recv()
+
+    def total(kind, rel, depth_of):
+        dy, dz, dx, _ = rel
+        value = ins[kind][slot_of(here, *rel)].astype(jnp.float32)
+        value = value + stage_in[kind][0][dy * 8 + dz * 2 + dx].astype(jnp.float32)
+        if depth_of >= 2:
+            value = value + stage_in[kind][1][dy * 4 + dz].astype(jnp.float32)
+        if depth_of >= 3:
+            value = value + stage_in[kind][2][dz].astype(jnp.float32)
+        return value
+
+    columns = [pl.ds(pl.multiple_of(side * 2 * part + y * part, 128), part) for side in range(2)]
+    near = pl.ds(pl.multiple_of(y * depth, depth), depth)
+    far = pl.ds(pl.multiple_of((1 - y) * depth, depth), depth)
+    locals_ = [
+        pltpu.make_async_copy(
+            grad_ref.at[near, pl.ds(side * part, part)],
+            grad_out.at[:, columns[side]],
+            local.at[side],
+        )
+        for side in range(2)
+    ]
+    for one in locals_:
+        one.start()
+    greet(here)
+    turns = (2, 1, 3, 0)
+    for dx in (1, 0):
+        for dy in (1, 0):
+            for dz in turns:
+                for kind in range(2):
+                    source = ins[kind].at[slot_of(here, dy, dz, dx, 1)]
+                    go(kind, 0, dy * 8 + dz * 2 + dx, source, (0, 0, 0, 1))
+    swaps = []
+    for side in range(2):
+        swaps.append(
+            pltpu.make_async_remote_copy(
+                src_ref=grad_ref.at[far, pl.ds(side * part, part)],
+                dst_ref=grad_out.at[:, columns[side]],
+                send_sem=g_send.at[side],
+                recv_sem=g_recv.at[side],
+                device_id=place_of(here, 1, 0, 0, 0),
+                device_id_type=MESH,
+            )
+        )
+        swaps[-1].start()
+    for dy in (1, 0):
+        for dz in turns:
+            for kind in range(2):
+                landed(kind, 0, dy * 8 + dz * 2 + 1)
+                out = stage_out[kind][1]
+                out[dy * 4 + dz] = total(kind, (dy, dz, 1, 0), 1).astype(out.dtype)
+                go(kind, 1, dy * 4 + dz, out.at[dy * 4 + dz], (0, 0, 1, 0))
+    for dz in turns:
+        for kind in range(2):
+            landed(kind, 0, 8 + dz * 2)
+            landed(kind, 1, 4 + dz)
+            out = stage_out[kind][2]
+            out[dz] = total(kind, (1, dz, 0, 0), 2).astype(out.dtype)
+            go(kind, 2, dz, out.at[dz], (1, 0, 0, 0))
+    for dz in turns:
+        for kind in range(2):
+            landed(kind, 0, dz * 2)
+            landed(kind, 1, dz)
+            landed(kind, 2, dz)
+            if dz:
+                out = stage_out[kind][3]
+                out[dz - 1] = total(kind, (0, dz, 0, 0), 3).astype(out.dtype)
+                go(kind, 3, dz - 1, out.at[dz - 1], (0, dz, 0, 0))
+    for kind in range(2):
+        value = total(kind, (0, 0, 0, 0), 3)
+        for index in range(3):
+            landed(kind, 3, index)
+            value = value + stage_in[kind][3][index].astype(jnp.float32)
+        result = (dx_out, dg_out)[kind]
+        result[...] = value.astype(result.dtype)
+    for one in sent:
+        one.wait_send()
+    for one in swaps:
+        one.wait()
+    for one in locals_:
+        one.wait()
+
+
+def merge_all(dx, dg, grad):
+    rows, width = dx.shape[1:]
+    depth, columns = grad.shape
+    vmem = pl.BlockSpec(memory_space=pltpu.VMEM)
+    whole = pl.BlockSpec(memory_space=pl.ANY)
+    wide = [pltpu.VMEM((n, rows, width), jnp.bfloat16) for n in (16, 8, 4, 3, 8, 4, 3)]
+    small = [pltpu.VMEM((n,) + dg.shape[1:], jnp.float32) for n in (16, 8, 4, 3, 8, 4, 3)]
+    return pl.pallas_call(
+        merge_kernel,
+        out_shape=(
+            jax.ShapeDtypeStruct((rows, width), jnp.bfloat16),
+            jax.ShapeDtypeStruct(dg.shape[1:], jnp.float32),
+            jax.ShapeDtypeStruct((depth // 2, 2 * columns), jnp.bfloat16),
+        ),
+        in_specs=[vmem, vmem, whole],
+        out_specs=(vmem, vmem, whole),
+        scratch_shapes=wide
+        + small
+        + [
+            pltpu.SemaphoreType.DMA((2, 31)),
+            pltpu.SemaphoreType.DMA((2, 31)),
+            pltpu.SemaphoreType.DMA((2,)),
+            pltpu.SemaphoreType.DMA((2,)),
+            pltpu.SemaphoreType.DMA((2,)),
+        ],
+        compiler_params=pltpu.CompilerParams(
+            collective_id=1, has_side_effects=True, vmem_limit_bytes=40 * 1024 * 1024
+        ),
+        name="merge_all",
+    )(dx, dg, grad)
+
+
 def partial_body(
     tokens,
     cotangent,
@@ -247,41 +587,27 @@
     fresh_out,
 ):
     micro, rows, width = tokens.shape
-    replicas = lax.axis_size("rep")
-    sources = lax.axis_size("exp")
-    devices = replicas * sources
-    num_exp = sources
+    num_exp = lax.axis_size("exp")
     hidden = w_in.shape[2] // 2
-    part = hidden // replicas
-    me_rep = lax.axis_index("rep")
+    part = hidden // lax.axis_size("rep")
     me_exp = lax.axis_index("exp")
     scale_in = 1.0 / math.sqrt(width)
     scale_out = 1.0 / math.sqrt(hidden)
-    both = ("rep", "exp")
-    swap = [(0, 1), (1, 0)]
-    depth = w_in.shape[1]
-
-    columns = w_in[0].reshape(depth, 2, replicas, part)
-    mine = lax.dynamic_index_in_dim(columns, me_rep, 2, keepdims=False).reshape(depth, 2 * part)
-    theirs = lax.dynamic_index_in_dim(columns, 1 - me_rep, 2, keepdims=False).reshape(
-        depth, 2 * part
-    )
-    got = lax.ppermute(theirs, "rep", swap)
-    low = me_rep == 0
-    weight_in = jnp.concatenate([jnp.where(low, mine, got), jnp.where(low, got, mine)], axis=0)
     weight_out = w_out[0]
-
-    chosen = routes[..., None] == jnp.arange(num_exp, dtype=jnp.int32)
-    spread = jnp.sum(jnp.where(chosen, gates[..., None], 0).astype(jnp.float32), axis=2)
-    all_gates = lax.all_gather(spread.astype(jnp.bfloat16), both, axis=0)
-    all_tokens = lax.all_gather(tokens, both, axis=0).reshape(-1, width)
-    all_cots = lax.all_gather(cotangent, both, axis=0).reshape(-1, width)
-    is_me = jnp.arange(num_exp, dtype=jnp.int32) == me_exp
-    gate = jnp.sum(
-        jnp.where(is_me, all_gates.reshape(-1, num_exp).astype(jnp.float32), 0.0),
-        axis=1,
-        keepdims=True,
-    )
+    own_rows = micro * rows
+    lanes = 128
+
+    chosen = routes.reshape(own_rows, -1, 1) == jnp.arange(num_exp, dtype=jnp.int32)
+    held_gates = gates.reshape(own_rows, -1, 1).astype(jnp.float32)
+    spread = jnp.sum(jnp.where(chosen, held_gates, 0.0), axis=1).T
+    spread = jnp.pad(spread, ((0, 0), (0, lanes - own_rows))).astype(jnp.bfloat16)
+    all_tokens, all_cots, all_gates, weight_in = spread_all(
+        tokens.reshape(own_rows, width), cotangent.reshape(own_rows, width), spread, w_in
+    )
+    all_tokens = all_tokens.reshape(-1, width)
+    all_cots = all_cots.reshape(-1, width)
+    gate = lax.dynamic_index_in_dim(all_gates, me_exp, 1, keepdims=False)[:, :own_rows]
+    gate = gate.astype(jnp.float32).reshape(-1, 1)
 
     pre = jnp.dot(all_tokens, weight_in, preferred_element_type=jnp.float32) * scale_in
     half, up = pre[:, :part], pre[:, part:]
@@ -305,35 +631,29 @@
         )
         * scale_in
     ).astype(jnp.bfloat16)
-    sides = grad_in.reshape(replicas, depth, 2 * part)
-    own_side = lax.dynamic_index_in_dim(sides, me_rep, 0, keepdims=False)
-    far_side = lax.dynamic_index_in_dim(sides, 1 - me_rep, 0, keepdims=False)
-    came = lax.ppermute(far_side, "rep", swap)
     rows_dx = (
         lax.dot_general(
             pre_cot, weight_in, (((1,), (1,)), ((), ())), preferred_element_type=jnp.float32
         )
         * scale_in
     ).astype(jnp.bfloat16)
-    token_dx = lax.psum_scatter(
-        rows_dx.reshape(devices, micro, rows, width), both, scatter_dimension=0, tiled=False
-    )
-    dense = jnp.where(is_me, gate_grad[:, None], 0.0).reshape(devices, micro * rows * num_exp)
-    token_gate = lax.psum_scatter(dense, both, scatter_dimension=0, tiled=False)
-    token_gate = token_gate.reshape(micro, rows, 1, num_exp)
-    d_gates = jnp.sum(jnp.where(chosen, token_gate, 0.0), axis=3).astype(jnp.bfloat16)
+    is_me = jnp.arange(num_exp, dtype=jnp.int32)[:, None] == me_exp
+    dense = jnp.pad(gate_grad.reshape(-1, 1, own_rows), ((0, 0), (0, 0), (0, lanes - own_rows)))
+    dense = jnp.where(is_me, dense, 0.0)
+    token_dx, token_gate, full_grad = merge_all(
+        rows_dx.reshape(-1, own_rows, width), dense, grad_in
+    )
+    token_dx = token_dx.reshape(micro, rows, width)
+    token_gate = token_gate[:, :own_rows].T[:, None, :]
+    d_gates = jnp.sum(jnp.where(chosen, token_gate, 0.0), axis=2).astype(jnp.bfloat16)
+    d_gates = d_gates.reshape(gates.shape)
     grad_out = (
         lax.dot_general(
             gated, all_cots, (((0,), (0,)), ((), ())), preferred_element_type=jnp.float32
         )
         * scale_out
     )[None]
-    first_cols = jnp.where(low, own_side, came)
-    last_cols = jnp.where(low, came, own_side)
-    full_grad = jnp.concatenate(
-        [first_cols[:, :part], last_cols[:, :part], first_cols[:, part:], last_cols[:, part:]],
-        axis=1,
-    )[None].astype(jnp.float32)
+    full_grad = full_grad[None].astype(jnp.float32)
     dead_flag = collapsed.reshape(-1, 1, 1)
     updated_in = adam_update(w_in, first_in, second_in, full_grad, fresh_in, dead_flag)
     updated_out = adam_update(w_out, first_out, second_out, grad_out, fresh_out, dead_flag)
@@ -350,7 +670,8 @@
 
 
 def solution(mesh):
-    inner = partial_body if mesh.shape["rep"] == 2 else body
+    narrow = mesh.shape["rep"] == 2 and mesh.shape["exp"] == 16
+    inner = partial_body if narrow else body
     placed = (
         P(None, ("rep", "exp"), None),
         P(None, ("rep", "exp"), None),

time: 439 us -> 214 us (0.49); the launches traced: 431 us -> 214 us
  waiting for transfers between devices: 240 us -> 0 us
  Pallas kernels: 0 us -> 156 us
  local copies, waits for them, and re-layouts: 64.6 us -> 7.36 us
  blocking collectives: 43.1 us -> 0 us
  matrix products: 51.6 us -> 37 us
  between operations: 15 us -> 1.45 us
  starting transfers between devices: 4.89 us -> 0 us
    pallas_call x0 -> x2, Pallas kernels: none -> 156 us  [the longest x1 93.4 us: spread_all(): pl.pallas_call(spread_kernel, out_shape=(jax.ShapeDtypeStruct((32, rows,...]
    reduce_scatter x1 -> x0, waiting for transfers between devices: 105 us -> none  [partial_body(): lax.psum_scatter(rows_dx.reshape(devices, micro, rows, width), both, scat...]
    all_gather x2 -> x0, waiting for transfers between devices: 64.9 us -> none  [the longest x1 62 us: partial_body(): all_cots = lax.all_gather(cotangent, both, axis=0).reshape(-1, width)]
    unnamed x5 -> x0, waiting for transfers between devices: 64.1 us -> none
    dynamic_slice x4 -> x1, local copies, waits for them, and re-layouts: 45.6 us -> 0.87 us  [partial_body(): lax.dynamic_index_in_dim(all_gates, me_exp, 1, keepdims=False)[:, :own_rows]]
    all_gather x1 -> x0, blocking collectives: 43.1 us -> none  [partial_body(): all_gates = lax.all_gather(spread.astype(jnp.bfloat16), both, axis=0)]
    another operation x1 -> x0, local copies, waits for them, and re-layouts: 6.22 us -> none  [partial_body(): columns = w_in[0].reshape(depth, 2, replicas, part)]
    ppermute x2 -> x0, waiting for transfers between devices: 5.95 us -> none  [the longest x1 5.95 us: partial_body(): got = lax.ppermute(theirs, 'rep', swap)]
  transfers between devices with their start and end apart: 6 -> 0, of which waited for: 5 -> 0; matrix products, arithmetic and copies ran while one was open for 26% -> 0% of each run, Pallas kernels for 0% -> 0%
where the time goes in v2:
time: 214 us
  Pallas kernels  156 us (73%)
  matrix products  37 us (17%)
  other arithmetic  12.1 us (6%)
  local copies, waits for them, and re-layouts  7.36 us (3%)
    pallas_call x1, Pallas kernels, spread_all(): pl.pallas_call(spread_kernel, out_shape=(jax.ShapeDtypeStruct((32, rows,...  93.4 us
    pallas_call x1, Pallas kernels, merge_all(): pl.pallas_call(merge_kernel, out_shape=(jax.ShapeDtypeStruct((rows, width...  62.4 us
    convert_element_type x1, other arithmetic, adam_update(): jnp.where(alive_mask, second_new, jnp.zeros_like(second_new))  11.9 us
    dot_general x1, matrix products, partial_body(): lax.dot_general(gated, all_cots, (((0,), (0,)), ((), ())), preferred_elem...  11.4 us
    dot_general x1, matrix products, partial_body(): jnp.dot(all_tokens, weight_in, preferred_element_type=jnp.float32)  8.48 us
    dot_general x1, matrix products, partial_body(): lax.dot_general(pre_cot, weight_in, (((1,), (1,)), ((), ())), preferred_e...  7.08 us
    dot_general x1, matrix products, partial_body(): lax.dot_general(all_tokens, pre_cot, (((0,), (0,)), ((), ())), preferred_...  5.34 us
    unnamed x24, local copies, waits for them, and re-layouts  4.8 us

profile of v2, /device:TPU:0, one launch (start us, length us, event | category | flops | bytes accessed | tf_op | source)
XLA Modules:
  0.0 213.8 jit_solution(7134788551864570651)
XLA Ops:
  0.6 0.7 copy.28
  1.3 0.1 eq.29
  1.4 0.7 copy.29
  2.1 0.1 reshape.81
  2.2 0.6 pad.9.gate_ref
  2.8 93.4 %spread_all.1 = (bf16[32,48,2048]{2,1,0:T(8,128)(2,1)}, bf16[32,48,2048]{2,1,0:T(8,128)(2,1)}, bf16[32,16,128]{2,1,0:T(8,128)(2,1)}, bf16[2048,768]{1,0:T(8,128)(2,1)}) custom-call(bf16[48,2048]{1,0:T(8,128)(2,1)} %bitcast.64, bf16[48,2048]{1,0:T(8,128)(2,1)} %bitcast.65, bf16[16,128]{1,0:T(8,128)(2,1)} %pad.9.gate_ref, bf16[1,1024,1536]{2,1,0:T(8,128)(2,1)} %w_ref.1), custom_call_target="tpu_custom_call" | custom-call | tf_op jit(solution)/shard_map/spread_all/pallas_call | solution.py:381
  96.2 0.9 constant_dynamic-slice_fusion
  97.1 0.1 reshape.82
  97.2 0.0 copy-start.4
  97.2 0.0 copy-start.7
  97.2 8.5 %convolution_multiply_fusion = f32[1536,768]{0,1:T(8,128)S(1)} fusion(bf16[1536,2048]{1,0:T(8,128)(2,1)} %bitcast.70, bf16[2048,768]{1,0:T(8,128)(2,1)} %get-tuple-element.18), kind=kOutput, calls=%fused_computation.11 | convolution fusion | flops 4833017856 | bytes 14155776 | tf_op jit(solution)/shard_map/dot_general | solution.py:612
  105.7 0.0 copy-done.4
  105.7 0.0 copy-done.7
  105.7 0.0 copy-start.5
  105.7 4.7 %fusion.4 = (f32[1536]{0:T(1024)S(1)}, bf16[1536,384]{0,1:T(8,128)(2,1)}, bf16[1536,384]{0,1:T(8,128)(2,1)S(1)}, bf16[1536,384]{0,1:T(8,128)(2,1)S(1)}) fusion(f32[1536,768]{0,1:T(8,128)S(1)} %convolution_multiply_fusion, f32[1536]{0:T(1024)S(1)} %broadcast_multiply_fusion, bf16[1536,2048]{1,0:T(8,128)(2,1)S(1)} %bitcast.69, ...), kind=kOutput, calls=%fused_computation.19 | convolution fusion | flops 2427714048 | bytes 16134144 | tf_op jit(solution)/shard_map/dot_general | solution.py:617
  110.4 0.0 copy-done.5
  110.4 0.0 copy-start.6
  110.4 5.3 %multiply_convert_fusion.1.grad_ref = bf16[2048,768]{1,0:T(8,128)(2,1)S(1)} fusion(bf16[1536,2048]{1,0:T(8,128)(2,1)S(1)} %bitcast.71, bf16[1536,384]{0,1:T(8,128)(2,1)S(1)} %get-tuple-element.42, bf16[1536,384]{0,1:T(8,128)(2,1)S(1)} %get-tuple-element.43), kind=kOutput, calls=%fused_computation.10 | convolution fusion | flops 4839702528 | bytes 11796480 | tf_op jit(solution)/shard_map/dot_general | solution.py:629
  115.8 0.0 copy-done.6
  115.8 7.1 %multiply_convert_fusion = bf16[1536,2048]{1,0:T(8,128)(2,1)} fusion(bf16[2048,768]{1,0:T(8,128)(2,1)S(1)} %copy-done.6, bf16[1536,384]{0,1:T(8,128)(2,1)S(1)} %get-tuple-element.42, bf16[1536,384]{0,1:T(8,128)(2,1)S(1)} %get-tuple-element.43), kind=kOutput, calls=%fused_computation | convolution fusion | flops 4842848256 | bytes 11796480 | tf_op jit(solution)/shard_map/dot_general | solution.py:635
  122.9 0.1 reshape.79
  123.0 0.1 broadcast_select_fusion.dg_ref
  123.1 0.0 copy-start
  123.1 2.8 %copy-done = bf16[1536,2048]{1,0:T(8,128)(2,1)S(1)} copy-done((bf16[1536,2048]{1,0:T(8,128)(2,1)S(1)}, bf16[1536,2048]{1,0:T(8,128)(2,1)}, u32[]{:S(2)}) %copy-start) | copy-done | bytes 6291480
  125.9 0.0 copy-start.1
  125.9 0.0 copy-start.2
  125.9 0.0 copy-start.3
  125.9 62.4 %merge_all.1 = (bf16[48,2048]{1,0:T(8,128)(2,1)S(1)}, f32[16,128]{1,0:T(8,128)S(1)}, bf16[1024,1536]{1,0:T(8,128)(2,1)S(1)}) custom-call(bf16[32,48,2048]{2,1,0:T(8,128)(2,1)S(1)} %bitcast.62, f32[32,16,128]{2,1,0:T(8,128)S(1)} %broadcast_select_fusion.dg_ref, bf16[2048,768]{1,0:T(8,128)(2,1)S(1)} %multiply_convert_fusion.1.grad_ref), custom_call_target="tpu_custom_call" | custom-call | tf_op jit(solution)/shard_map/merge_all/pallas_call | solution.py:549
  189.0 0.0 copy-done.1
  189.0 0.0 copy-done.2
  189.0 0.0 copy-done.3
  189.0 0.0 copy-start.8
  189.0 0.0 copy-start.9
  189.0 11.9 %select_convert_fusion = (bf16[1,1024,1536]{2,1,0:T(8,128)(2,1)}, bf16[1,1024,1536]{2,1,0:T(8,128)(2,1)}, bf16[1,1024,1536]{2,1,0:T(8,128)(2,1)}) fusion(bf16[1024,1536]{1,0:T(8,128)(2,1)S(1)} %get-tuple-element.21, bf16[1,1024,1536]{2,1,0:T(8,128)(2,1)S(1)} %copy-done.2, pred[]{:T(512)} %bitcast.10, bf16[1,1024,1536]{2,1,0:T(8,128)(2,1)S(1)} %copy-done.3, ...), kind=kLoop, calls=%fused_computation.7 | loop fusion | flops 36175872 | bytes 25165824 | tf_op jit(solution)/shard_map/convert_element_type | solution.py:68
  201.0 0.1 convert_element_type.94
  201.1 0.6 copy.30
  201.7 0.0 copy-done.8
  201.7 0.0 copy-done.9
  201.7 11.4 %select_convert_fusion.3 = (bf16[1,384,2048]{2,1,0:T(8,128)(2,1)}, bf16[1,384,2048]{2,1,0:T(8,128)(2,1)}, bf16[1,384,2048]{2,1,0:T(8,128)(2,1)}) fusion(bf16[1,384,2048]{2,1,0:T(8,128)(2,1)S(1)} %copy-done.9, pred[]{:T(512)} %bitcast.10, bf16[1,384,2048]{2,1,0:T(8,128)(2,1)} %param.25, bf16[1,384,2048]{2,1,0:T(8,128)(2,1)} %param.22, ...), kind=kOutput, calls=%fused_computation.14 | convolution fusion | flops 2435776512 | bytes 18487296 | tf_op jit(solution)/shard_map/dot_general | solution.py:651
  213.1 0.7 copy.36
  (8 shorter events, 0.1 us)
Async XLA Ops:
  97.2 8.5 %copy-start.4 = (bf16[32,48,2048]{2,1,0:T(8,128)(2,1)S(1)}, bf16[32,48,2048]{2,1,0:T(8,128)(2,1)}, u32[]{:S(2)}) copy-start(bf16[32,48,2048]{2,1,0:T(8,128)(2,1)} %get-tuple-element.15) | copy-start | bytes 18874372
  97.2 8.5 %copy-start.7 = (bf16[1,384,2048]{2,1,0:T(8,128)(2,1)S(1)}, bf16[1,384,2048]{2,1,0:T(8,128)(2,1)}, u32[]{:S(2)}) copy-start(bf16[1,384,2048]{2,1,0:T(8,128)(2,1)} %param.19) | copy-start | bytes 4718596
  105.7 4.7 %copy-start.5 = (bf16[32,48,2048]{2,1,0:T(8,128)(2,1)S(1)}, bf16[32,48,2048]{2,1,0:T(8,128)(2,1)}, u32[]{:S(2)}) copy-start(bf16[32,48,2048]{2,1,0:T(8,128)(2,1)} %get-tuple-element.17) | copy-start | bytes 18874372
  110.4 5.4 %copy-start.6 = (bf16[2048,768]{1,0:T(8,128)(2,1)S(1)}, bf16[2048,768]{1,0:T(8,128)(2,1)}, u32[]{:S(2)}) copy-start(bf16[2048,768]{1,0:T(8,128)(2,1)} %get-tuple-element.18) | copy-start | bytes 9437188
  123.1 2.8 %copy-start = (bf16[1536,2048]{1,0:T(8,128)(2,1)S(1)}, bf16[1536,2048]{1,0:T(8,128)(2,1)}, u32[]{:S(2)}) copy-start(bf16[1536,2048]{1,0:T(8,128)(2,1)} %multiply_convert_fusion) | copy-start | bytes 18874372
  125.9 63.1 %copy-start.1 = (bf16[1,1024,1536]{2,1,0:T(8,128)(2,1)S(1)}, bf16[1,1024,1536]{2,1,0:T(8,128)(2,1)}, u32[]{:S(2)}) copy-start(bf16[1,1024,1536]{2,1,0:T(8,128)(2,1)} %w_ref.1) | copy-start | bytes 9437188
  125.9 63.1 %copy-start.2 = (bf16[1,1024,1536]{2,1,0:T(8,128)(2,1)S(1)}, bf16[1,1024,1536]{2,1,0:T(8,128)(2,1)}, u32[]{:S(2)}) copy-start(bf16[1,1024,1536]{2,1,0:T(8,128)(2,1)} %param.21) | copy-start | bytes 9437188
  125.9 63.1 %copy-start.3 = (bf16[1,1024,1536]{2,1,0:T(8,128)(2,1)S(1)}, bf16[1,1024,1536]{2,1,0:T(8,128)(2,1)}, u32[]{:S(2)}) copy-start(bf16[1,1024,1536]{2,1,0:T(8,128)(2,1)} %param.24) | copy-start | bytes 9437188
  189.0 12.7 %copy-start.8 = (bf16[1,384,2048]{2,1,0:T(8,128)(2,1)S(1)}, bf16[1,384,2048]{2,1,0:T(8,128)(2,1)}, u32[]{:S(2)}) copy-start(bf16[1,384,2048]{2,1,0:T(8,128)(2,1)} %param.19) | copy-start | bytes 4718596
  189.0 12.7 %copy-start.9 = (bf16[1,384,2048]{2,1,0:T(8,128)(2,1)S(1)}, bf16[1,384,2048]{2,1,0:T(8,128)(2,1)}, u32[]{:S(2)}) copy-start(bf16[1,384,2048]{2,1,0:T(8,128)(2,1)} %param.23) | copy-start | bytes 4718596

commit v3 on v2

--- a/solution.py
+++ b/solution.py
@@ -297,11 +297,11 @@
             goes = []
             if dx == 0:
                 goes.append(((0, 0, 1, 0), (dy, dz, 1, 0)))
-            if dx == 0 and dy == 0:
+            if dx == 0 and dy == 0 and (kind != 1 or dz == 0):
                 goes.append(((1, 0, 0, 0), (1, dz, 0, 0)))
-            if rel == own:
+            if rel == own or (kind == 1 and dx == 0 and dz == 0):
                 for step in (1, 3, 2):
-                    goes.append(((0, Z_SIDE - step, 0, 0), (0, step, 0, 0)))
+                    goes.append(((0, Z_SIDE - step, 0, 0), (dy, step, 0, 0)))
             goes.append(((0, 0, 0, 1), (dy, dz, dx, 1)))
             for target, arrives in goes:
                 one = copy(kind, rel, target, arrives)
@@ -434,7 +434,7 @@
     ins = (dx_ref, dg_ref)
     stage_in = ((r1x, r2x, r3x, r4x), (r1g, r2g, r3g, r4g))
     stage_out = ((None, s2x, s3x, s4x), (None, s2g, s3g, s4g))
-    firsts = (0, 16, 24, 28)
+    firsts = (0, 16, 24, 30)
 
     def copy(kind, stage, index, source, target):
         return pltpu.make_async_remote_copy(
@@ -464,7 +464,8 @@
         if depth_of >= 2:
             value = value + stage_in[kind][1][dy * 4 + dz].astype(jnp.float32)
         if depth_of >= 3:
-            value = value + stage_in[kind][2][dz].astype(jnp.float32)
+            for index in range(3):
+                value = value + stage_in[kind][2][dy * 3 + index].astype(jnp.float32)
         return value
 
     columns = [pl.ds(pl.multiple_of(side * 2 * part + y * part, 128), part) for side in range(2)]
@@ -481,13 +482,12 @@
     for one in locals_:
         one.start()
     greet(here)
-    turns = (2, 1, 3, 0)
+    turns = ((1, 2), (1, 1), (1, 3), (0, 2), (0, 1), (0, 3), (1, 0), (0, 0))
     for dx in (1, 0):
-        for dy in (1, 0):
-            for dz in turns:
-                for kind in range(2):
-                    source = ins[kind].at[slot_of(here, dy, dz, dx, 1)]
-                    go(kind, 0, dy * 8 + dz * 2 + dx, source, (0, 0, 0, 1))
+        for dy, dz in turns:
+            for kind in range(2):
+                source = ins[kind].at[slot_of(here, dy, dz, dx, 1)]
+                go(kind, 0, dy * 8 + dz * 2 + dx, source, (0, 0, 0, 1))
     swaps = []
     for side in range(2):
         swaps.append(
@@ -501,34 +501,33 @@
             )
         )
         swaps[-1].start()
-    for dy in (1, 0):
-        for dz in turns:
-            for kind in range(2):
-                landed(kind, 0, dy * 8 + dz * 2 + 1)
-                out = stage_out[kind][1]
-                out[dy * 4 + dz] = total(kind, (dy, dz, 1, 0), 1).astype(out.dtype)
-                go(kind, 1, dy * 4 + dz, out.at[dy * 4 + dz], (0, 0, 1, 0))
-    for dz in turns:
+    for dy, dz in turns:
         for kind in range(2):
-            landed(kind, 0, 8 + dz * 2)
-            landed(kind, 1, 4 + dz)
-            out = stage_out[kind][2]
-            out[dz] = total(kind, (1, dz, 0, 0), 2).astype(out.dtype)
-            go(kind, 2, dz, out.at[dz], (1, 0, 0, 0))
-    for dz in turns:
+            landed(kind, 0, dy * 8 + dz * 2 + 1)
+            out = stage_out[kind][1]
+            out[dy * 4 + dz] = total(kind, (dy, dz, 1, 0), 1).astype(out.dtype)
+            go(kind, 1, dy * 4 + dz, out.at[dy * 4 + dz], (0, 0, 1, 0))
+    for dy, dz in turns:
         for kind in range(2):
-            landed(kind, 0, dz * 2)
-            landed(kind, 1, dz)
-            landed(kind, 2, dz)
+            landed(kind, 0, dy * 8 + dz * 2)
+            landed(kind, 1, dy * 4 + dz)
             if dz:
-                out = stage_out[kind][3]
-                out[dz - 1] = total(kind, (0, dz, 0, 0), 3).astype(out.dtype)
-                go(kind, 3, dz - 1, out.at[dz - 1], (0, dz, 0, 0))
+                index = dy * 3 + dz - 1
+                out = stage_out[kind][2]
+                out[index] = total(kind, (dy, dz, 0, 0), 2).astype(out.dtype)
+                go(kind, 2, index, out.at[index], (0, dz, 0, 0))
     for kind in range(2):
+        for index in range(3):
+            landed(kind, 2, 3 + index)
+        out = stage_out[kind][3]
+        out[0] = total(kind, (1, 0, 0, 0), 3).astype(out.dtype)
+        go(kind, 3, 0, out.at[0], (1, 0, 0, 0))
+    for kind in range(2):
+        for index in range(3):
+            landed(kind, 2, index)
         value = total(kind, (0, 0, 0, 0), 3)
-        for index in range(3):
-            landed(kind, 3, index)
-            value = value + stage_in[kind][3][index].astype(jnp.float32)
+        landed(kind, 3, 0)
+        value = value + stage_in[kind][3][0].astype(jnp.float32)
         result = (dx_out, dg_out)[kind]
         result[...] = value.astype(result.dtype)
     for one in sent:
@@ -544,8 +543,8 @@
     depth, columns = grad.shape
     vmem = pl.BlockSpec(memory_space=pltpu.VMEM)
     whole = pl.BlockSpec(memory_space=pl.ANY)
-    wide = [pltpu.VMEM((n, rows, width), jnp.bfloat16) for n in (16, 8, 4, 3, 8, 4, 3)]
-    small = [pltpu.VMEM((n,) + dg.shape[1:], jnp.float32) for n in (16, 8, 4, 3, 8, 4, 3)]
+    wide = [pltpu.VMEM((n, rows, width), jnp.bfloat16) for n in (16, 8, 6, 1, 8, 6, 1)]
+    small = [pltpu.VMEM((n,) + dg.shape[1:], jnp.float32) for n in (16, 8, 6, 1, 8, 6, 1)]
     return pl.pallas_call(
         merge_kernel,
         out_shape=(

time: 214 us -> 201 us (0.939)
  Pallas kernels: 156 us -> 143 us
    pallas_call x1, Pallas kernels: 62.4 us -> 50.6 us  [merge_all(): pl.pallas_call(merge_kernel, out_shape=(jax.ShapeDtypeStruct((rows, width...]
where the time goes in v3:
time: 201 us
  Pallas kernels  143 us (71%)
  matrix products  37 us (18%)
  other arithmetic  12.1 us (6%)
  local copies, waits for them, and re-layouts  7.36 us (4%)
    pallas_call x1, Pallas kernels, spread_all(): pl.pallas_call(spread_kernel, out_shape=(jax.ShapeDtypeStruct((32, rows,...  92.6 us
    pallas_call x1, Pallas kernels, merge_all(): pl.pallas_call(merge_kernel, out_shape=(jax.ShapeDtypeStruct((rows, width...  50.6 us
    convert_element_type x1, other arithmetic, adam_update(): jnp.where(alive_mask, second_new, jnp.zeros_like(second_new))  11.9 us
    dot_general x1, matrix products, partial_body(): lax.dot_general(gated, all_cots, (((0,), (0,)), ((), ())), preferred_elem...  11.4 us
    dot_general x1, matrix products, partial_body(): jnp.dot(all_tokens, weight_in, preferred_element_type=jnp.float32)  8.48 us
    dot_general x1, matrix products, partial_body(): lax.dot_general(pre_cot, weight_in, (((1,), (1,)), ((), ())), preferred_e...  7.08 us
    dot_general x1, matrix products, partial_body(): lax.dot_general(all_tokens, pre_cot, (((0,), (0,)), ((), ())), preferred_...  5.34 us
    unnamed x24, local copies, waits for them, and re-layouts  4.8 us

profile of v3, /device:TPU:0, one launch (start us, length us, event | category | flops | bytes accessed | tf_op | source)
XLA Modules:
  0.0 201.1 jit_solution(6647419427336901847)
XLA Ops:
  0.6 0.7 copy.28
  1.3 0.1 eq.29
  1.4 0.7 copy.29
  2.1 0.1 reshape.81
  2.2 0.6 pad.9.gate_ref
  2.8 92.6 %spread_all.1 = (bf16[32,48,2048]{2,1,0:T(8,128)(2,1)}, bf16[32,48,2048]{2,1,0:T(8,128)(2,1)}, bf16[32,16,128]{2,1,0:T(8,128)(2,1)}, bf16[2048,768]{1,0:T(8,128)(2,1)}) custom-call(bf16[48,2048]{1,0:T(8,128)(2,1)} %bitcast.64, bf16[48,2048]{1,0:T(8,128)(2,1)} %bitcast.65, bf16[16,128]{1,0:T(8,128)(2,1)} %pad.9.gate_ref, bf16[1,1024,1536]{2,1,0:T(8,128)(2,1)} %w_ref.1), custom_call_target="tpu_custom_call" | custom-call | tf_op jit(solution)/shard_map/spread_all/pallas_call | solution.py:381
  95.4 0.9 constant_dynamic-slice_fusion
  96.3 0.1 reshape.82
  96.4 0.0 copy-start.4
  96.4 0.0 copy-start.7
  96.4 8.5 %convolution_multiply_fusion = f32[1536,768]{0,1:T(8,128)S(1)} fusion(bf16[1536,2048]{1,0:T(8,128)(2,1)} %bitcast.70, bf16[2048,768]{1,0:T(8,128)(2,1)} %get-tuple-element.18), kind=kOutput, calls=%fused_computation.11 | convolution fusion | flops 4833017856 | bytes 14155776 | tf_op jit(solution)/shard_map/dot_general | solution.py:611
  104.9 0.0 copy-done.4
  104.9 0.0 copy-done.7
  104.9 0.0 copy-start.5
  105.0 4.7 %fusion.4 = (f32[1536]{0:T(1024)S(1)}, bf16[1536,384]{0,1:T(8,128)(2,1)}, bf16[1536,384]{0,1:T(8,128)(2,1)S(1)}, bf16[1536,384]{0,1:T(8,128)(2,1)S(1)}) fusion(f32[1536,768]{0,1:T(8,128)S(1)} %convolution_multiply_fusion, f32[1536]{0:T(1024)S(1)} %broadcast_multiply_fusion, bf16[1536,2048]{1,0:T(8,128)(2,1)S(1)} %bitcast.69, ...), kind=kOutput, calls=%fused_computation.19 | convolution fusion | flops 2427714048 | bytes 16134144 | tf_op jit(solution)/shard_map/dot_general | solution.py:616
  109.7 0.0 copy-done.5
  109.7 0.0 copy-start.6
  109.7 5.3 %multiply_convert_fusion.1.grad_ref = bf16[2048,768]{1,0:T(8,128)(2,1)S(1)} fusion(bf16[1536,2048]{1,0:T(8,128)(2,1)S(1)} %bitcast.71, bf16[1536,384]{0,1:T(8,128)(2,1)S(1)} %get-tuple-element.42, bf16[1536,384]{0,1:T(8,128)(2,1)S(1)} %get-tuple-element.43), kind=kOutput, calls=%fused_computation.10 | convolution fusion | flops 4839702528 | bytes 11796480 | tf_op jit(solution)/shard_map/dot_general | solution.py:628
  115.0 0.0 copy-done.6
  115.0 7.1 %multiply_convert_fusion = bf16[1536,2048]{1,0:T(8,128)(2,1)} fusion(bf16[2048,768]{1,0:T(8,128)(2,1)S(1)} %copy-done.6, bf16[1536,384]{0,1:T(8,128)(2,1)S(1)} %get-tuple-element.42, bf16[1536,384]{0,1:T(8,128)(2,1)S(1)} %get-tuple-element.43), kind=kOutput, calls=%fused_computation | convolution fusion | flops 4842848256 | bytes 11796480 | tf_op jit(solution)/shard_map/dot_general | solution.py:634
  122.1 0.1 reshape.79
  122.2 0.1 broadcast_select_fusion.dg_ref
  122.3 0.0 copy-start
  122.3 2.8 %copy-done = bf16[1536,2048]{1,0:T(8,128)(2,1)S(1)} copy-done((bf16[1536,2048]{1,0:T(8,128)(2,1)S(1)}, bf16[1536,2048]{1,0:T(8,128)(2,1)}, u32[]{:S(2)}) %copy-start) | copy-done | bytes 6291480
  125.1 0.0 copy-start.1
  125.1 0.0 copy-start.2
  125.1 0.0 copy-start.3
  125.1 50.6 %merge_all.1 = (bf16[48,2048]{1,0:T(8,128)(2,1)S(1)}, f32[16,128]{1,0:T(8,128)S(1)}, bf16[1024,1536]{1,0:T(8,128)(2,1)S(1)}) custom-call(bf16[32,48,2048]{2,1,0:T(8,128)(2,1)S(1)} %bitcast.62, f32[32,16,128]{2,1,0:T(8,128)S(1)} %broadcast_select_fusion.dg_ref, bf16[2048,768]{1,0:T(8,128)(2,1)S(1)} %multiply_convert_fusion.1.grad_ref), custom_call_target="tpu_custom_call" | custom-call | tf_op jit(solution)/shard_map/merge_all/pallas_call | solution.py:548
  176.3 0.0 copy-done.1
  176.3 0.0 copy-done.2
  176.3 0.0 copy-done.3
  176.3 0.0 copy-start.8
  176.3 0.0 copy-start.9
  176.4 11.9 %select_convert_fusion = (bf16[1,1024,1536]{2,1,0:T(8,128)(2,1)}, bf16[1,1024,1536]{2,1,0:T(8,128)(2,1)}, bf16[1,1024,1536]{2,1,0:T(8,128)(2,1)}) fusion(bf16[1024,1536]{1,0:T(8,128)(2,1)S(1)} %get-tuple-element.21, bf16[1,1024,1536]{2,1,0:T(8,128)(2,1)S(1)} %copy-done.2, pred[]{:T(512)} %bitcast.10, bf16[1,1024,1536]{2,1,0:T(8,128)(2,1)S(1)} %copy-done.3, ...), kind=kLoop, calls=%fused_computation.7 | loop fusion | flops 36175872 | bytes 25165824 | tf_op jit(solution)/shard_map/convert_element_type | solution.py:68
  188.3 0.1 convert_element_type.94
  188.4 0.6 copy.30
  189.0 0.0 copy-done.8
  189.0 0.0 copy-done.9
  189.0 11.4 %select_convert_fusion.3 = (bf16[1,384,2048]{2,1,0:T(8,128)(2,1)}, bf16[1,384,2048]{2,1,0:T(8,128)(2,1)}, bf16[1,384,2048]{2,1,0:T(8,128)(2,1)}) fusion(bf16[1,384,2048]{2,1,0:T(8,128)(2,1)S(1)} %copy-done.9, pred[]{:T(512)} %bitcast.10, bf16[1,384,2048]{2,1,0:T(8,128)(2,1)} %param.25, bf16[1,384,2048]{2,1,0:T(8,128)(2,1)} %param.22, ...), kind=kOutput, calls=%fused_computation.14 | convolution fusion | flops 2435776512 | bytes 18487296 | tf_op jit(solution)/shard_map/dot_general | solution.py:650
  200.4 0.7 copy.36
  (8 shorter events, 0.1 us)
Async XLA Ops:
  96.4 8.5 %copy-start.4 = (bf16[32,48,2048]{2,1,0:T(8,128)(2,1)S(1)}, bf16[32,48,2048]{2,1,0:T(8,128)(2,1)}, u32[]{:S(2)}) copy-start(bf16[32,48,2048]{2,1,0:T(8,128)(2,1)} %get-tuple-element.15) | copy-start | bytes 18874372
  96.4 8.5 %copy-start.7 = (bf16[1,384,2048]{2,1,0:T(8,128)(2,1)S(1)}, bf16[1,384,2048]{2,1,0:T(8,128)(2,1)}, u32[]{:S(2)}) copy-start(bf16[1,384,2048]{2,1,0:T(8,128)(2,1)} %param.19) | copy-start | bytes 4718596
  104.9 4.7 %copy-start.5 = (bf16[32,48,2048]{2,1,0:T(8,128)(2,1)S(1)}, bf16[32,48,2048]{2,1,0:T(8,128)(2,1)}, u32[]{:S(2)}) copy-start(bf16[32,48,2048]{2,1,0:T(8,128)(2,1)} %get-tuple-element.17) | copy-start | bytes 18874372
  109.7 5.4 %copy-start.6 = (bf16[2048,768]{1,0:T(8,128)(2,1)S(1)}, bf16[2048,768]{1,0:T(8,128)(2,1)}, u32[]{:S(2)}) copy-start(bf16[2048,768]{1,0:T(8,128)(2,1)} %get-tuple-element.18) | copy-start | bytes 9437188
  122.3 2.8 %copy-start = (bf16[1536,2048]{1,0:T(8,128)(2,1)S(1)}, bf16[1536,2048]{1,0:T(8,128)(2,1)}, u32[]{:S(2)}) copy-start(bf16[1536,2048]{1,0:T(8,128)(2,1)} %multiply_convert_fusion) | copy-start | bytes 18874372
  125.1 51.2 %copy-start.1 = (bf16[1,1024,1536]{2,1,0:T(8,128)(2,1)S(1)}, bf16[1,1024,1536]{2,1,0:T(8,128)(2,1)}, u32[]{:S(2)}) copy-start(bf16[1,1024,1536]{2,1,0:T(8,128)(2,1)} %w_ref.1) | copy-start | bytes 9437188
  125.1 51.2 %copy-start.2 = (bf16[1,1024,1536]{2,1,0:T(8,128)(2,1)S(1)}, bf16[1,1024,1536]{2,1,0:T(8,128)(2,1)}, u32[]{:S(2)}) copy-start(bf16[1,1024,1536]{2,1,0:T(8,128)(2,1)} %param.21) | copy-start | bytes 9437188
  125.1 51.2 %copy-start.3 = (bf16[1,1024,1536]{2,1,0:T(8,128)(2,1)S(1)}, bf16[1,1024,1536]{2,1,0:T(8,128)(2,1)}, u32[]{:S(2)}) copy-start(bf16[1,1024,1536]{2,1,0:T(8,128)(2,1)} %param.24) | copy-start | bytes 9437188
  176.3 12.7 %copy-start.8 = (bf16[1,384,2048]{2,1,0:T(8,128)(2,1)S(1)}, bf16[1,384,2048]{2,1,0:T(8,128)(2,1)}, u32[]{:S(2)}) copy-start(bf16[1,384,2048]{2,1,0:T(8,128)(2,1)} %param.19) | copy-start | bytes 4718596
  176.3 12.7 %copy-start.9 = (bf16[1,384,2048]{2,1,0:T(8,128)(2,1)S(1)}, bf16[1,384,2048]{2,1,0:T(8,128)(2,1)}, u32[]{:S(2)}) copy-start(bf16[1,384,2048]{2,1,0:T(8,128)(2,1)} %param.23) | copy-start | bytes 4718596

commit v4 on v3

--- a/solution.py
+++ b/solution.py
@@ -351,7 +351,6 @@
                 device_id_type=MESH,
             )
         )
-        swaps[-1].start()
     order = [(1, 0, 0, 0), (0, 1, 0, 0), (0, 3, 0, 0), (0, 0, 1, 0), (1, 1, 0, 0), (1, 3, 0, 0)]
     order += [(0, 2, 0, 0), (1, 0, 1, 0), (1, 2, 0, 0)]
     for dz in (1, 3, 2):
@@ -361,6 +360,9 @@
         for kind in range(3):
             landed(kind, rel)
             pass_on(rel, (kind,))
+        if rel == order[0]:
+            for one in swaps:
+                one.start()
     for dy in range(2):
         for dz in range(Z_SIDE):
             for dx in range(2):

time: 201 us -> 201 us (level)
  no operation moved by 1% of the time
where the time goes in v4:
time: 201 us
  Pallas kernels  143 us (71%)
  matrix products  37 us (18%)
  other arithmetic  12.1 us (6%)
  local copies, waits for them, and re-layouts  7.36 us (4%)
    pallas_call x1, Pallas kernels, spread_all(): pl.pallas_call(spread_kernel, out_shape=(jax.ShapeDtypeStruct((32, rows,...  92.6 us
    pallas_call x1, Pallas kernels, merge_all(): pl.pallas_call(merge_kernel, out_shape=(jax.ShapeDtypeStruct((rows, width...  50.6 us
    convert_element_type x1, other arithmetic, adam_update(): jnp.where(alive_mask, second_new, jnp.zeros_like(second_new))  11.9 us
    dot_general x1, matrix products, partial_body(): lax.dot_general(gated, all_cots, (((0,), (0,)), ((), ())), preferred_elem...  11.4 us
    dot_general x1, matrix products, partial_body(): jnp.dot(all_tokens, weight_in, preferred_element_type=jnp.float32)  8.48 us
    dot_general x1, matrix products, partial_body(): lax.dot_general(pre_cot, weight_in, (((1,), (1,)), ((), ())), preferred_e...  7.08 us
    dot_general x1, matrix products, partial_body(): lax.dot_general(all_tokens, pre_cot, (((0,), (0,)), ((), ())), preferred_...  5.34 us
    unnamed x24, local copies, waits for them, and re-layouts  4.8 us

profile of v4, /device:TPU:0, one launch (start us, length us, event | category | flops | bytes accessed | tf_op | source)
XLA Modules:
  0.0 201.1 jit_solution(18269987199595453320)
XLA Ops:
  0.6 0.7 copy.28
  1.3 0.1 eq.29
  1.4 0.7 copy.29
  2.1 0.1 reshape.81
  2.2 0.6 pad.9.gate_ref
  2.8 92.6 %spread_all.1 = (bf16[32,48,2048]{2,1,0:T(8,128)(2,1)}, bf16[32,48,2048]{2,1,0:T(8,128)(2,1)}, bf16[32,16,128]{2,1,0:T(8,128)(2,1)}, bf16[2048,768]{1,0:T(8,128)(2,1)}) custom-call(bf16[48,2048]{1,0:T(8,128)(2,1)} %bitcast.64, bf16[48,2048]{1,0:T(8,128)(2,1)} %bitcast.65, bf16[16,128]{1,0:T(8,128)(2,1)} %pad.9.gate_ref, bf16[1,1024,1536]{2,1,0:T(8,128)(2,1)} %w_ref.1), custom_call_target="tpu_custom_call" | custom-call | tf_op jit(solution)/shard_map/spread_all/pallas_call | solution.py:383
  95.4 0.9 constant_dynamic-slice_fusion
  96.3 0.1 reshape.82
  96.4 0.0 copy-start.4
  96.4 0.0 copy-start.7
  96.4 8.5 %convolution_multiply_fusion = f32[1536,768]{0,1:T(8,128)S(1)} fusion(bf16[1536,2048]{1,0:T(8,128)(2,1)} %bitcast.70, bf16[2048,768]{1,0:T(8,128)(2,1)} %get-tuple-element.18), kind=kOutput, calls=%fused_computation.11 | convolution fusion | flops 4833017856 | bytes 14155776 | tf_op jit(solution)/shard_map/dot_general | solution.py:613
  104.9 0.0 copy-done.4
  104.9 0.0 copy-done.7
  104.9 0.0 copy-start.5
  104.9 4.7 %fusion.4 = (f32[1536]{0:T(1024)S(1)}, bf16[1536,384]{0,1:T(8,128)(2,1)}, bf16[1536,384]{0,1:T(8,128)(2,1)S(1)}, bf16[1536,384]{0,1:T(8,128)(2,1)S(1)}) fusion(f32[1536,768]{0,1:T(8,128)S(1)} %convolution_multiply_fusion, f32[1536]{0:T(1024)S(1)} %broadcast_multiply_fusion, bf16[1536,2048]{1,0:T(8,128)(2,1)S(1)} %bitcast.69, ...), kind=kOutput, calls=%fused_computation.19 | convolution fusion | flops 2427714048 | bytes 16134144 | tf_op jit(solution)/shard_map/dot_general | solution.py:618
  109.7 0.0 copy-done.5
  109.7 0.0 copy-start.6
  109.7 5.3 %multiply_convert_fusion.1.grad_ref = bf16[2048,768]{1,0:T(8,128)(2,1)S(1)} fusion(bf16[1536,2048]{1,0:T(8,128)(2,1)S(1)} %bitcast.71, bf16[1536,384]{0,1:T(8,128)(2,1)S(1)} %get-tuple-element.42, bf16[1536,384]{0,1:T(8,128)(2,1)S(1)} %get-tuple-element.43), kind=kOutput, calls=%fused_computation.10 | convolution fusion | flops 4839702528 | bytes 11796480 | tf_op jit(solution)/shard_map/dot_general | solution.py:630
  115.0 0.0 copy-done.6
  115.0 7.1 %multiply_convert_fusion = bf16[1536,2048]{1,0:T(8,128)(2,1)} fusion(bf16[2048,768]{1,0:T(8,128)(2,1)S(1)} %copy-done.6, bf16[1536,384]{0,1:T(8,128)(2,1)S(1)} %get-tuple-element.42, bf16[1536,384]{0,1:T(8,128)(2,1)S(1)} %get-tuple-element.43), kind=kOutput, calls=%fused_computation | convolution fusion | flops 4842848256 | bytes 11796480 | tf_op jit(solution)/shard_map/dot_general | solution.py:636
  122.1 0.1 reshape.79
  122.2 0.1 broadcast_select_fusion.dg_ref
  122.3 0.0 copy-start
  122.3 2.8 %copy-done = bf16[1536,2048]{1,0:T(8,128)(2,1)S(1)} copy-done((bf16[1536,2048]{1,0:T(8,128)(2,1)S(1)}, bf16[1536,2048]{1,0:T(8,128)(2,1)}, u32[]{:S(2)}) %copy-start) | copy-done | bytes 6291480
  125.1 0.0 copy-start.1
  125.1 0.0 copy-start.2
  125.1 0.0 copy-start.3
  125.1 50.6 %merge_all.1 = (bf16[48,2048]{1,0:T(8,128)(2,1)S(1)}, f32[16,128]{1,0:T(8,128)S(1)}, bf16[1024,1536]{1,0:T(8,128)(2,1)S(1)}) custom-call(bf16[32,48,2048]{2,1,0:T(8,128)(2,1)S(1)} %bitcast.62, f32[32,16,128]{2,1,0:T(8,128)S(1)} %broadcast_select_fusion.dg_ref, bf16[2048,768]{1,0:T(8,128)(2,1)S(1)} %multiply_convert_fusion.1.grad_ref), custom_call_target="tpu_custom_call" | custom-call | tf_op jit(solution)/shard_map/merge_all/pallas_call | solution.py:550
  176.3 0.0 copy-done.1
  176.3 0.0 copy-done.2
  176.3 0.0 copy-done.3
  176.3 0.0 copy-start.8
  176.3 0.0 copy-start.9
  176.4 11.9 %select_convert_fusion = (bf16[1,1024,1536]{2,1,0:T(8,128)(2,1)}, bf16[1,1024,1536]{2,1,0:T(8,128)(2,1)}, bf16[1,1024,1536]{2,1,0:T(8,128)(2,1)}) fusion(bf16[1024,1536]{1,0:T(8,128)(2,1)S(1)} %get-tuple-element.21, bf16[1,1024,1536]{2,1,0:T(8,128)(2,1)S(1)} %copy-done.2, pred[]{:T(512)} %bitcast.10, bf16[1,1024,1536]{2,1,0:T(8,128)(2,1)S(1)} %copy-done.3, ...), kind=kLoop, calls=%fused_computation.7 | loop fusion | flops 36175872 | bytes 25165824 | tf_op jit(solution)/shard_map/convert_element_type | solution.py:68
  188.3 0.1 convert_element_type.94
  188.4 0.6 copy.30
  189.0 0.0 copy-done.8
  189.0 0.0 copy-done.9
  189.0 11.4 %select_convert_fusion.3 = (bf16[1,384,2048]{2,1,0:T(8,128)(2,1)}, bf16[1,384,2048]{2,1,0:T(8,128)(2,1)}, bf16[1,384,2048]{2,1,0:T(8,128)(2,1)}) fusion(bf16[1,384,2048]{2,1,0:T(8,128)(2,1)S(1)} %copy-done.9, pred[]{:T(512)} %bitcast.10, bf16[1,384,2048]{2,1,0:T(8,128)(2,1)} %param.25, bf16[1,384,2048]{2,1,0:T(8,128)(2,1)} %param.22, ...), kind=kOutput, calls=%fused_computation.14 | convolution fusion | flops 2435776512 | bytes 18487296 | tf_op jit(solution)/shard_map/dot_general | solution.py:652
  200.4 0.7 copy.36
  (8 shorter events, 0.1 us)
Async XLA Ops:
  96.4 8.5 %copy-start.4 = (bf16[32,48,2048]{2,1,0:T(8,128)(2,1)S(1)}, bf16[32,48,2048]{2,1,0:T(8,128)(2,1)}, u32[]{:S(2)}) copy-start(bf16[32,48,2048]{2,1,0:T(8,128)(2,1)} %get-tuple-element.15) | copy-start | bytes 18874372
  96.4 8.5 %copy-start.7 = (bf16[1,384,2048]{2,1,0:T(8,128)(2,1)S(1)}, bf16[1,384,2048]{2,1,0:T(8,128)(2,1)}, u32[]{:S(2)}) copy-start(bf16[1,384,2048]{2,1,0:T(8,128)(2,1)} %param.19) | copy-start | bytes 4718596
  104.9 4.7 %copy-start.5 = (bf16[32,48,2048]{2,1,0:T(8,128)(2,1)S(1)}, bf16[32,48,2048]{2,1,0:T(8,128)(2,1)}, u32[]{:S(2)}) copy-start(bf16[32,48,2048]{2,1,0:T(8,128)(2,1)} %get-tuple-element.17) | copy-start | bytes 18874372
  109.7 5.4 %copy-start.6 = (bf16[2048,768]{1,0:T(8,128)(2,1)S(1)}, bf16[2048,768]{1,0:T(8,128)(2,1)}, u32[]{:S(2)}) copy-start(bf16[2048,768]{1,0:T(8,128)(2,1)} %get-tuple-element.18) | copy-start | bytes 9437188
  122.3 2.8 %copy-start = (bf16[1536,2048]{1,0:T(8,128)(2,1)S(1)}, bf16[1536,2048]{1,0:T(8,128)(2,1)}, u32[]{:S(2)}) copy-start(bf16[1536,2048]{1,0:T(8,128)(2,1)} %multiply_convert_fusion) | copy-start | bytes 18874372
  125.1 51.2 %copy-start.1 = (bf16[1,1024,1536]{2,1,0:T(8,128)(2,1)S(1)}, bf16[1,1024,1536]{2,1,0:T(8,128)(2,1)}, u32[]{:S(2)}) copy-start(bf16[1,1024,1536]{2,1,0:T(8,128)(2,1)} %w_ref.1) | copy-start | bytes 9437188
  125.1 51.2 %copy-start.2 = (bf16[1,1024,1536]{2,1,0:T(8,128)(2,1)S(1)}, bf16[1,1024,1536]{2,1,0:T(8,128)(2,1)}, u32[]{:S(2)}) copy-start(bf16[1,1024,1536]{2,1,0:T(8,128)(2,1)} %param.21) | copy-start | bytes 9437188
  125.1 51.2 %copy-start.3 = (bf16[1,1024,1536]{2,1,0:T(8,128)(2,1)S(1)}, bf16[1,1024,1536]{2,1,0:T(8,128)(2,1)}, u32[]{:S(2)}) copy-start(bf16[1,1024,1536]{2,1,0:T(8,128)(2,1)} %param.24) | copy-start | bytes 9437188
  176.3 12.7 %copy-start.8 = (bf16[1,384,2048]{2,1,0:T(8,128)(2,1)S(1)}, bf16[1,384,2048]{2,1,0:T(8,128)(2,1)}, u32[]{:S(2)}) copy-start(bf16[1,384,2048]{2,1,0:T(8,128)(2,1)} %param.19) | copy-start | bytes 4718596
  176.3 12.7 %copy-start.9 = (bf16[1,384,2048]{2,1,0:T(8,128)(2,1)S(1)}, bf16[1,384,2048]{2,1,0:T(8,128)(2,1)}, u32[]{:S(2)}) copy-start(bf16[1,384,2048]{2,1,0:T(8,128)(2,1)} %param.23) | copy-start | bytes 4718596
